TPU v7x, 128 devices: a whole 4x4x4 slice. The times are simulated.
128 devices in a mesh: seq: 32 (over x, z, core), head: 4 (over y).
Axes of the slice: x: 4, y: 4, z: 4, core: 2. Of those that a mesh axis runs over, the one named last changes fastest.
Arguments:
- tokens: bfloat16 [12288, 2240], P('seq'), may hold values from -40 to 40
- w_query: bfloat16 [2240, 2240], P(None, 'head'), may hold values from -0.125 to 0.125
- w_key: bfloat16 [2240, 2240], P(None, 'head'), may hold values from -0.125 to 0.125
- w_value: bfloat16 [2240, 2240], P(None, 'head'), may hold values from -0.125 to 0.125
- w_out: bfloat16 [2240, 2240], P('head'), may hold values from -0.125 to 0.125
- grad_out: bfloat16 [12288, 2240], P('seq'), may hold values from -6 to 6
Outputs:
- attn_out: bfloat16 [12288, 2240], P('seq', 'head')
- grad_tokens: bfloat16 [12288, 2240], P('seq', 'head')
- grad_query: float32 [2240, 2240], P('seq', 'head')
- grad_key: float32 [2240, 2240], P('seq', 'head')
- grad_value: float32 [2240, 2240], P('seq', 'head')
- grad_wout: float32 [2240, 2240], P('head', 'seq')
All inputs are finite; a program needn't handle non-finite values.
Results may differ from a plain program's by a relative error of at most 0.018.
Values sent between devices are 32-bit elements; how exact they have to be, the bound alone decides.
A program may use at most 128 MiB of HBM per device.

v0:
```python
import math

import jax
import jax.numpy as jnp
from jax import lax
from jax.sharding import PartitionSpec as P

HEAD_DIM = 112


epsilon = 1e-15
exact = lax.Precision.HIGHEST


def body(tokens, w_query, w_key, w_value, w_out, grad_out):
    f32 = jnp.float32
    tok_rows = tokens.shape[0]
    local_width = w_query.shape[1]
    head_count = local_width // HEAD_DIM
    queries = jax.nn.relu(jnp.dot(tokens, w_query, preferred_element_type=f32)).astype(jnp.bfloat16)
    key_feat = jax.nn.relu(jnp.dot(tokens, w_key, preferred_element_type=f32)).astype(jnp.bfloat16)
    val_feat = jnp.dot(tokens, w_value, preferred_element_type=f32).astype(jnp.bfloat16)
    query_heads = queries.astype(f32).reshape(tok_rows, head_count, HEAD_DIM)
    key_heads = key_feat.astype(f32).reshape(tok_rows, head_count, HEAD_DIM)
    value_heads = val_feat.astype(f32).reshape(tok_rows, head_count, HEAD_DIM)
    state_part = jnp.einsum("thc,the->hce", key_heads, value_heads, precision=exact)
    ksum_part = jnp.sum(key_heads, axis=0)
    kv_state, key_sum = lax.psum((state_part, ksum_part), "seq")
    numerator = jnp.einsum("thc,hce->the", query_heads, kv_state, precision=exact)
    denominator = jnp.einsum("thc,hc->th", query_heads, key_sum, precision=exact) + epsilon
    attended = numerator / denominator[..., None]
    mixed = attended.reshape(tok_rows, local_width).astype(jnp.bfloat16)
    partial_out = jnp.dot(mixed, w_out, preferred_element_type=f32)
    attn_out = lax.psum_scatter(partial_out, "head", scatter_dimension=1, tiled=True).astype(
        jnp.bfloat16
    )
    grad_mixed = jnp.einsum("td,cd->tc", grad_out, w_out, preferred_element_type=f32).astype(
        jnp.bfloat16
    )
    upstream = grad_mixed.astype(f32).reshape(tok_rows, head_count, HEAD_DIM)
    num_grad = upstream / denominator[..., None]
    den_grad = -jnp.sum(upstream * attended, axis=-1) / denominator
    gstate_part = jnp.einsum("thc,the->hce", query_heads, num_grad, precision=exact)
    gksum_part = jnp.einsum("th,thc->hc", den_grad, query_heads, precision=exact)
    grad_state, grad_ksum = lax.psum((gstate_part, gksum_part), "seq")
    dq_full = (
        jnp.einsum("the,hce->thc", num_grad, kv_state, precision=exact)
        + den_grad[..., None] * key_sum[None]
    )
    dk_full = jnp.einsum("the,hce->thc", value_heads, grad_state, precision=exact) + grad_ksum[None]
    dv_full = jnp.einsum("thc,hce->the", key_heads, grad_state, precision=exact)
    dq_pre = (
        jnp.where(query_heads > 0, dq_full, 0.0).reshape(tok_rows, local_width).astype(jnp.bfloat16)
    )
    dk_pre = (
        jnp.where(key_heads > 0, dk_full, 0.0).reshape(tok_rows, local_width).astype(jnp.bfloat16)
    )
    dv_pre = dv_full.reshape(tok_rows, local_width).astype(jnp.bfloat16)
    partial_in = (
        jnp.einsum("tc,dc->td", dq_pre, w_query, preferred_element_type=f32)
        + jnp.einsum("tc,dc->td", dk_pre, w_key, preferred_element_type=f32)
        + jnp.einsum("tc,dc->td", dv_pre, w_value, preferred_element_type=f32)
    )
    grad_tokens = lax.psum_scatter(partial_in, "head", scatter_dimension=1, tiled=True).astype(
        jnp.bfloat16
    )
    factor = 1.0 / math.sqrt(tok_rows * lax.axis_size("seq"))
    stacked = jnp.concatenate([dq_pre, dk_pre, dv_pre], axis=1)
    whole_term = jnp.einsum("tr,tc->rc", tokens, stacked, preferred_element_type=f32)
    summed = lax.psum_scatter(whole_term, "seq", scatter_dimension=0, tiled=True)
    summed = summed * factor
    grad_query = summed[:, :local_width]
    grad_key = summed[:, local_width : 2 * local_width]
    grad_value = summed[:, 2 * local_width :]
    out_term = jnp.einsum("tc,td->cd", mixed, grad_out, preferred_element_type=f32)
    grad_wout = lax.psum_scatter(out_term, "seq", scatter_dimension=1, tiled=True) * factor
    return (attn_out, grad_tokens, grad_query, grad_key, grad_value, grad_wout)


def solution(mesh):
    in_specs = (
        P("seq", None),
        P(None, "head"),
        P(None, "head"),
        P(None, "head"),
        P("head", None),
        P("seq", None),
    )
    out_specs = (
        P("seq", "head"),
        P("seq", "head"),
        P("seq", "head"),
        P("seq", "head"),
        P("seq", "head"),
        P("head", "seq"),
    )
    return jax.shard_map(body, mesh=mesh, in_specs=in_specs, out_specs=out_specs, check_vma=False)
```

profile of v0, /device:TPU:0, one launch (start us, length us, event | category | flops | bytes accessed | tf_op | source)
XLA Modules:
  0.0 505.1 jit_solution(11478763131178172409)
XLA Ops:
  7.3 4.6 convolution_convert_fusion.2
  11.9 1.6 convert_reduce_fusion
  13.6 68.4 %psum.29 = f32[5,112]{1,0:T(8,128)S(1)} all-reduce(f32[5,112]{1,0:T(8,128)S(1)} %reduce_sum.21), channel_id=1, replica_groups=mesh['seq'=32,'head'=4] {'seq'}, use_global_device_ids=true, to_apply=%region_2.3 | all-reduce | flops 560 | bytes 4480 | tf_op jit(solution)/shard_map/psum | solution.py:28
  82.0 3.8 convert_compare_fusion.1
  86.2 1.5 convolution_convert_fusion.1
  87.7 1.0 fusion.27
  88.7 1.5 fusion.16
  90.3 98.6 %all-reduce.9.cloned.1.call-done = (f32[5,112,112]{2,1,0:T(8,128)}, f32[5,112,112]{2,1,0:T(8,128)}) async-done(((f32[5,112,112]{2,1,0:T(8,128)}, f32[5,112,112]{2,1,0:T(8,128)}), (f32[5,112,112]{2,1,0:T(8,128)}, f32[5,112,112]{2,1,0:T(8,128)})) %all-reduce.9.cloned.1.call-update) | async-done | bytes 501776 | tf_op jit(solution)/shard_map/psum | solution.py:28
  188.9 1.9 fusion.15
  191.5 3.6 fusion.28
  196.6 66.9 %psum.31 = f32[5,112]{1,0:T(8,128)S(1)} all-reduce(f32[5,112]{1,0:T(8,128)S(1)} %bitcast.102), channel_id=1, replica_groups=mesh['seq'=32,'head'=4] {'seq'}, use_global_device_ids=true, to_apply=%region_6.7 | all-reduce | flops 560 | bytes 4480 | tf_op jit(solution)/shard_map/psum | solution.py:45
  263.5 1.5 convolution_convert_fusion
  265.0 1.7 fusion.13
  266.7 2.1 fusion.14
  268.9 1.9 fusion.29
  270.8 1.9 convolution_add_fusion.1
  272.7 3.7 convolution_add_fusion
  276.5 1.4 copy-done.8
  278.0 9.1 %convolution_bitcast_fusion = f32[2240,1680]{0,1:T(8,128)} fusion(bf16[384,2240]{0,1:T(8,128)(2,1)S(1)} %copy-done.8, bf16[384,560]{0,1:T(8,128)(2,1)S(1)} %bitcast.87, bf16[384,560]{0,1:T(8,128)(2,1)S(1)} %bitcast.93, bf16[384,560]{0,1:T(8,128)(2,1)S(1)} %bitcast.99), kind=kOutput, calls=%fused_computation | convolution fusion | flops 2894008320 | bytes 18063360 | tf_op jit(solution)/shard_map/tr,tc->rc/dot_general | solution.py:69
  287.1 1.4 copy-done.6
  288.6 4.2 fusion.30
  292.9 85.8 %fusion = f32[560,80]{0,1:T(8,128)S(1)} fusion(f32[560,2240]{0,1:T(8,128)} %fusion.30), kind=kCustom, calls=%all-reduce-scatter | all-reduce-scatter fusion | flops 1433601 | bytes 5197312
  378.7 1.3 collective-permute-start.2
  380.0 1.3 collective-permute-start.1
  381.3 1.3 collective-permute-start
  382.6 1.3 collective-permute-start.3
  385.9 9.8 %collective-permute-done.3 = f32[560,70]{0,1:T(8,128)S(1)} collective-permute-done((f32[560,70]{0,1:T(8,128)S(1)}, f32[560,70]{0,1:T(8,128)S(1)}, u32[]{:S(2)}, u32[]{:S(2)}) %collective-permute-start.3) | collective-permute-done | bytes 156832
  395.6 1.0 concatenate.4
  397.3 2.0 convert_element_type.59
  399.3 2.1 convert_element_type.69
  401.4 92.9 %all-reduce.7.cloned.1.call-done = f32[2240,1680]{0,1:T(8,128)} async-done(((f32[2240,1680]{0,1:T(8,128)}), f32[2240,1680]{0,1:T(8,128)}) %all-reduce.7.cloned.1.call-update) | async-done | bytes 15052816
  494.3 1.7 dynamic-slice_multiply_fusion
  (61 shorter events, 6.9 us)
Async XLA Ops:
  7.2 74.8 %copy-start = (bf16[2240,560]{0,1:T(8,128)(2,1)S(1)}, bf16[2240,560]{0,1:T(8,128)(2,1)}, u32[]{:S(2)}) copy-start(bf16[2240,560]{0,1:T(8,128)(2,1)} %param.7) | copy-start | bytes 7526404
  7.2 181.7 %all-reduce.9.cloned.1.call-start = ((), (), s32[]{:S(2)}) async-start(), calls=%async_computation.5 | async-start | bytes 1146880 | tf_op jit(solution)/shard_map/psum | solution.py:28
  7.2 4.7 copy-start.2
  7.2 4.7 copy-start.7
  82.0 4.2 copy-start.5
  82.0 4.1 copy-start.15
  86.2 1.5 copy-start.11
  87.7 1.0 copy-start.17
  90.2 307.1 %reduce-scatter.6.cloned.1.call-start = ((), (), s32[]{:S(2)}) async-start(), calls=%async_computation.2 | async-start | bytes 4300800 | tf_op jit(solution)/shard_map/reduce_scatter | solution.py:34
  188.9 2.7 copy-start.16
  190.8 0.8 copy-start.9
  195.2 204.1 %reduce-scatter.8.cloned.1.call-start = ((), (), s32[]{:S(2)}) async-start(), calls=%async_computation.3 | async-start | bytes 4300800 | tf_op jit(solution)/shard_map/reduce_scatter | solution.py:64
  268.9 1.9 copy-start.12
  268.9 1.9 copy-start.3
  270.8 1.9 copy-start.4
  276.4 1.5 copy-start.8
  276.4 1.5 copy-start.13
  276.5 217.8 %all-reduce.7.cloned.1.call-start = ((), (), s32[]{:S(2)}) async-start(), calls=%async_computation.4 | async-start | bytes 30965760
  287.1 1.5 copy-start.6
  287.1 1.5 copy-start.10
  292.9 91.1 %copy-start.14 = (u32[128]{0:T(128)S(1)}, u32[128]{0:T(128)}, u32[]{:S(2)}) copy-start(u32[128]{0:T(128)} %constant.13) | copy-start | bytes 1540
  378.7 16.9 %collective-permute-start.2 = (f32[560,80]{0,1:T(8,128)S(1)}, f32[560,80]{0,1:T(8,128)S(1)}, u32[]{:S(2)}, u32[]{:S(2)}) collective-permute-start(f32[560,80]{0,1:T(8,128)S(1)} %fusion), channel_id=1, source_target_pairs={{0,12},{4,16},{8,20},{12,24},{16,28},{20,32},{24,36},{28,40},{32,4... | collective-permute-start | bytes 537608
  380.0 15.6 %collective-permute-start.1 = (f32[560,80]{0,1:T(8,128)S(1)}, f32[560,80]{0,1:T(8,128)S(1)}, u32[]{:S(2)}, u32[]{:S(2)}) collective-permute-start(f32[560,80]{0,1:T(8,128)S(1)} %fusion), channel_id=1, source_target_pairs={{0,8},{4,12},{8,16},{12,20},{16,24},{20,28},{24,32},{28,36},{32,40... | collective-permute-start | bytes 537608
  381.3 14.3 %collective-permute-start = (f32[560,80]{0,1:T(8,128)S(1)}, f32[560,80]{0,1:T(8,128)S(1)}, u32[]{:S(2)}, u32[]{:S(2)}) collective-permute-start(f32[560,80]{0,1:T(8,128)S(1)} %fusion), channel_id=1, source_target_pairs={{0,4},{4,8},{8,12},{12,16},{16,20},{20,24},{24,28},{28,32},{32,36}... | collective-permute-start | bytes 537608
  382.6 13.0 %collective-permute-start.3 = (f32[560,70]{0,1:T(8,128)S(1)}, f32[560,70]{0,1:T(8,128)S(1)}, u32[]{:S(2)}, u32[]{:S(2)}) collective-permute-start(f32[560,70]{0,1:T(8,128)S(1)} %slice.15), channel_id=1, source_target_pairs={{0,16},{4,20},{8,24},{12,28},{16,32},{20,36},{24,40},{28,44},{32,4... | collective-permute-start | bytes 470408
  399.3 99.3 %copy-start.1 = (bf16[2240,560]{0,1:T(8,128)(2,1)S(1)}, bf16[2240,560]{0,1:T(8,128)(2,1)}, u32[]{:S(2)}) copy-start(bf16[2240,560]{0,1:T(8,128)(2,1)} %param.7) | copy-start | bytes 7526404
Sparse Core Ops, SparseCore 0:
  90.4 98.4 all-reduce.8
  195.3 40.9 reduce-scatter.5
  276.6 36.9 reduce-scatter.7
  317.0 177.2 all-reduce.6
where the time goes:
time: 506 us; the launch traced here: 505 us
  blocking collectives  221 us (44%)
  waiting for transfers between devices  201 us (40%)
  matrix products  46.6 us (9%)
  between operations  15.3 us (3%)
  local copies, waits for them, and re-layouts  8 us (2%)
  other arithmetic  7.36 us (1%)
  starting transfers between devices  5.37 us (1%)
    unnamed x9, waiting for transfers between devices  103 us
    psum x1, waiting for transfers between devices, body(): kv_state, key_sum = lax.psum((state_part, ksum_part), 'seq')  98.6 us
    unnamed x1, blocking collectives  85.8 us
    psum x1, blocking collectives, body(): kv_state, key_sum = lax.psum((state_part, ksum_part), 'seq')  68.4 us
    psum x1, blocking collectives, body(): grad_state, grad_ksum = lax.psum((gstate_part, gksum_part), 'seq')  66.9 us
  transfers between devices with their start and end apart: 8, of which 3 were waited for; matrix products, arithmetic and copies ran while one was open for 24% of the time, Pallas kernels for 0%

commit v1 on v0

v1 whole, which is shorter than its diff:
```python
import functools
import math

import jax
import jax.numpy as jnp
from jax import lax
from jax.experimental import pallas as pl
from jax.experimental.pallas import tpu as pltpu
from jax.sharding import PartitionSpec as P

f32 = jnp.float32
bf16 = jnp.bfloat16
MESH = pl.DeviceIdType.MESH

D = 2240
W = 560
WP = 640
T = 384
HD = 112
ROWS = 70
RP = 72
NB = 16
GR = NB * RP
GC = 1152
CH = 4 * RP
SR = 576
EPS = 1e-15


def dot(a, b):
    return lax.dot_general(a, b, (((1,), (0,)), ((), ())), preferred_element_type=f32)


def dot_t(a, b):
    return lax.dot_general(a, b, (((1,), (1,)), ((), ())), preferred_element_type=f32)


def dot_n(a, b):
    return lax.dot_general(a, b, (((0,), (0,)), ((), ())), preferred_element_type=f32)


def parts(v):
    high = v.astype(bf16)
    return high, (v - high.astype(f32)).astype(bf16)


def head_of(index):
    total = jnp.zeros_like(index)
    for edge in (112, 224, 336, 448, 560):
        total = total + (index >= edge).astype(jnp.int32)
    return total


def same_head(row0, rows, col0, cols):
    r = lax.broadcasted_iota(jnp.int32, (rows, cols), 0) + row0
    c = lax.broadcasted_iota(jnp.int32, (rows, cols), 1) + col0
    return head_of(r) == head_of(c)


def loop(count, fn):
    def step(i, carry):
        fn(i)
        return carry

    lax.fori_loop(0, count, step, 0)


class Copies:
    def __init__(self, send, recv):
        self.send, self.recv, self.used, self.open = send, recv, 0, []

    def start(self, src, dst, device):
        k = self.used
        self.used += 1
        copy = pltpu.make_async_remote_copy(
            src_ref=src, dst_ref=dst, send_sem=self.send.at[k], recv_sem=self.recv.at[k],
            device_id=device, device_id_type=MESH)
        copy.start()
        self.open.append(copy)
        return copy

    def sent(self, copy):
        copy.wait_send()
        self.open = [other for other in self.open if other is not copy]

    def finish(self):
        for copy in self.open:
            copy.wait_send()
        self.open = []


class Ring:
    def __init__(self, copies, left, right, slot, box, cut):
        self.copies, self.left, self.right, self.slot = copies, left, right, slot
        self.box, self.cut = box, cut
        self.rows = box.shape[1]

    def land(self, kind, half):
        if half == 0:
            return self.box.at[kind, pl.ds(0, self.cut), :]
        return self.box.at[kind, pl.ds(self.cut, self.rows - self.cut), :]

    def far(self):
        self.a0 = self.copies.start(self.slot("far", 0), self.land(0, 0), self.right)
        self.a1 = self.copies.start(self.slot("far", 1), self.land(0, 1), self.left)

    def near_right(self):
        self.d1 = self.copies.start(self.slot("right", 1), self.land(1, 1), self.right)

    def near_left(self):
        self.d0 = self.copies.start(self.slot("left", 0), self.land(1, 0), self.left)

    def combine(self):
        self.a0.wait_recv()
        ref = self.slot("right", 0)
        ref[...] = ref[...] + self.land(0, 0)[...]
        self.c0 = self.copies.start(ref, self.land(2, 0), self.right)
        self.a1.wait_recv()
        ref = self.slot("left", 1)
        ref[...] = ref[...] + self.land(0, 1)[...]
        self.c1 = self.copies.start(ref, self.land(2, 1), self.left)

    def arrived(self):
        for copy in (self.d0, self.d1, self.c0, self.c1):
            copy.wait_recv()

    def sent(self, names):
        for name in names:
            self.copies.sent(getattr(self, name))


def kernel(tok_h, wq_h, wk_h, wv_h, wo_h, go_h,
           at_o, gt_o, g1_o, g2_o,
           tok, go, wslot, wo, wot, tokt, got,
           q, k, v, gm, mx, ngh, ngl, dg, kvh, kvl, ones,
           send, recv, rhs, gbuf, own1, own2, box1, box2, pbox1, pbox2,
           cp, dp, cbox, dbox,
           sta, a0, a1, a2, afin, asum, stb, b0, b1, b2, bfin, bsum,
           in_sem, w_sem, out_sem, ssem, rsem):
    s = lax.axis_index("seq")
    y = lax.axis_index("head")
    c = s % 2
    chip = s // 2
    x = chip // 4
    z = chip % 4
    fa = x * (1 - c) + z * c
    sa = z * (1 - c) + x * c

    def first(i):
        return {"seq": ((i * (1 - c) + sa * c) * 4 + sa * (1 - c) + i * c) * 2 + c, "head": y}

    def second(i):
        return {"seq": ((fa * (1 - c) + i * c) * 4 + i * (1 - c) + fa * c) * 2 + c, "head": y}

    def along_y(i):
        return {"seq": s, "head": i}

    partner = {"seq": s + 1 - 2 * c, "head": y}

    def local(src, dst, sem):
        copy = pltpu.make_async_copy(src, dst, sem)
        copy.start()
        return copy

    in_tok = local(tok_h, tok, in_sem.at[0])
    in_k = local(wk_h, wslot.at[0], in_sem.at[1])
    in_v = local(wv_h, wslot.at[1], in_sem.at[2])
    in_go = local(go_h, go, in_sem.at[3])
    in_wo = local(wo_h, wo, in_sem.at[4])

    barrier = pltpu.get_barrier_semaphore()
    peers = [partner, along_y((y + 1) % 4), along_y((y + 3) % 4)]
    peers += [first((fa + d) % 4) for d in (1, 2, 3)]
    peers += [second((sa + d) % 4) for d in (1, 2, 3)]
    for peer in peers:
        pl.semaphore_signal(barrier, inc=1, device_id=peer, device_id_type=MESH)

    copies = Copies(ssem, rsem)

    for ref in (q, k, v, gm):
        ref[:, 512:WP] = jnp.zeros((T, WP - 512), bf16)

    def project(src, weight, dst, act):
        def tile(i):
            r = pl.ds(pl.multiple_of(i * 128, 128), 128)
            value = dot(src[r, :], weight[...])
            if act:
                value = jnp.maximum(value, 0.0)
            dst[r, 0:W] = value.astype(bf16)

        loop(T // 128, tile)

    def pack_state(st, left, rights, sums):
        for i in range(5):
            total = None
            for right in rights:
                block = dot_n(left[:, 128 * i:128 * i + 128], right[...])
                total = block if total is None else total + block
            total = jnp.where(same_head(128 * i, 128, 0, WP), total, 0.0)
            folded = total[:, 0:128]
            for j in range(1, 5):
                folded = folded + total[:, 128 * j:128 * j + 128]
            height = min(128, SR - 128 * i)
            st[128 * i:128 * i + height, :] = folded[:height, :]
        for j in range(5):
            st[W + j:W + j + 1, :] = sums[:, 128 * j:128 * j + 128]

    def unpack_state(fin):
        def tile(r0, rows, keep):
            block = fin[r0:r0 + rows, :]
            if keep < rows:
                block = jnp.where(lax.broadcasted_iota(jnp.int32, (rows, 128), 0) < keep, block, 0.0)
            for j in range(5):
                high, low = parts(jnp.where(same_head(r0, rows, 128 * j, 128), block, 0.0))
                kvh[r0:r0 + rows, 128 * j:128 * j + 128] = high
                kvl[r0:r0 + rows, 128 * j:128 * j + 128] = low

        for i in range(4):
            tile(128 * i, 128, 128)
        tile(512, 64, 48)

    def sums_row(fin):
        return jnp.concatenate([fin[W + j:W + j + 1, :] for j in range(5)], axis=1)

    half = SR // 2
    piece = half // 4
    mine = pl.multiple_of(c * half, 8)
    other = pl.multiple_of((1 - c) * half, 8)

    def mine_piece(i):
        return pl.ds(pl.multiple_of(c * half + i * piece, 8), piece)

    class State:
        def __init__(self, st, r0, r1, r2, fin, total):
            self.st, self.r0, self.r1, self.r2, self.fin, self.total = st, r0, r1, r2, fin, total

        def step0(self):
            self.c = copies.start(self.st.at[pl.ds(other, half), :], self.r0, partner)

        def step1(self):
            self.c.wait_recv()
            rows = pl.ds(mine, half)
            self.st[rows, :] = self.st[rows, :] + self.r0[...]
            self.cs = [copies.start(self.st.at[mine_piece((fa + d) % 4), :], self.r1.at[d - 1],
                                    first((fa + d) % 4)) for d in (1, 2, 3)]

        def step2(self):
            for copy in self.cs:
                copy.wait_recv()
            self.total[...] = (self.st[mine_piece(fa), :] + self.r1[0]) + (self.r1[1] + self.r1[2])
            self.cs = [copies.start(self.total, self.r2.at[d - 1], second((sa + d) % 4))
                       for d in (1, 2, 3)]

        def step3(self):
            for copy in self.cs:
                copy.wait_recv()
            rows = mine_piece(fa)
            self.fin[rows, :] = (self.total[...] + self.r2[0]) + (self.r2[1] + self.r2[2])
            self.cs = [copies.start(self.fin.at[rows, :], self.fin.at[rows, :], first((fa + d) % 4))
                       for d in (1, 2, 3)]

        def step4(self):
            for copy in self.cs:
                copy.wait_recv()
            rows = pl.ds(mine, half)
            self.c = copies.start(self.fin.at[rows, :], self.fin.at[rows, :], partner)

        def done(self):
            self.c.wait_recv()

    in_tok.wait()
    in_k.wait()
    project(tok, wslot.at[0], k, True)
    in_q = local(wq_h, wslot.at[0], in_sem.at[5])
    in_v.wait()
    project(tok, wslot.at[1], v, False)
    pack_state(sta, k, [v], jnp.sum(k[...].astype(f32), axis=0, keepdims=True))
    pl.semaphore_wait(barrier, len(peers))
    state = State(sta, a0, a1, a2, afin, asum)
    state.step0()

    in_q.wait()
    project(tok, wslot.at[0], q, True)
    state.step1()

    ring_y = {"far": (y + 2) % 4, "right": (y + 1) % 4, "left": (y + 3) % 4, "own": y}

    def fetch(which, place):
        rows = pl.ds(pl.multiple_of(ring_y[which] * W, 16), W)
        return [local(w.at[rows, :], wslot.at[place, pl.ds(W * i, W), :], w_sem.at[place, i])
                for i, w in enumerate((wq_h, wk_h, wv_h))]

    fetch_far = fetch("far", 0)
    fetch_right = fetch("right", 1)

    def gather_rows(src, base, which):
        for b in range(NB):
            lo = 2 * ROWS * b
            w0 = lo // 128 * 128
            w1 = min(D, -(-(lo + 2 * ROWS) // 128) * 128)
            i = lax.broadcasted_iota(jnp.int32, (RP, w1 - w0), 0)
            j = lax.broadcasted_iota(jnp.int32, (RP, w1 - w0), 1)
            pick = jnp.logical_and(j == i + (lo - w0) + ROWS * which, i < ROWS)
            value = dot_t(pick.astype(f32).astype(bf16), src[:, w0:w1])
            place = b * (1 - which) + (b % 4 * 4 + b // 4) * which
            cp[pl.ds(pl.multiple_of(base + place * RP, 8), RP), :] = value

    def rows_of(src, dst, base):
        gather_rows(src, base, c)

        def cast(i):
            r = pl.multiple_of(i * 288, 16)
            dst[pl.ds(r, 288), 0:T] = cp[pl.ds(pl.multiple_of(base + r, 8), 288), :].astype(bf16)

        loop(GR // 288, cast)
        gather_rows(src, base, 1 - c)
        place = pl.ds(base, GR)
        return copies.start(cp.at[place, :], dp.at[place, :], partner)

    send_tok = rows_of(tok, tokt, 0)
    state.step2()

    in_wo.wait()
    in_go.wait()

    def mixed_grad(i):
        r = pl.ds(pl.multiple_of(i * 128, 128), 128)
        gm[r, 0:W] = dot_t(go[r, :], wo[...]).astype(bf16)

    loop(T // 128, mixed_grad)
    state.step3()
    send_go = rows_of(go, got, GR)
    state.step4()

    for j in range(0, D, 256):
        n = min(256, D - j)
        eye = (lax.broadcasted_iota(jnp.int32, (n, n), 0) == lax.broadcasted_iota(jnp.int32, (n, n), 1))
        wot[j:j + n, :] = dot_t(eye.astype(f32).astype(bf16), wo[:, j:j + n]).astype(bf16)
    for i in range(5):
        ones[128 * i:128 * i + 128, :] = same_head(128 * i, 128, 0, WP).astype(f32).astype(bf16)
    kvh[SR:WP, :] = jnp.zeros((WP - SR, WP), bf16)
    kvl[SR:WP, :] = jnp.zeros((WP - SR, WP), bf16)

    state.done()
    unpack_state(afin)
    ksum = sums_row(afin)

    def attend(i):
        r = pl.ds(pl.multiple_of(i * 128, 128), 128)
        qt = q[r, :]
        num = dot(qt, kvh[...]) + dot(qt, kvl[...])
        high, low = parts(qt.astype(f32) * ksum)
        rec = 1.0 / (dot(high, ones[...]) + dot(low, ones[...]) + EPS)
        att = num * rec
        mx[r, :] = att.astype(bf16)
        g = gm[r, :].astype(f32)
        high, low = parts(g * rec)
        ngh[r, :] = high
        ngl[r, :] = low
        high, low = parts(g * att)
        dg[r, :] = -(dot(high, ones[...]) + dot(low, ones[...])) * rec

    loop(T // 128, attend)

    send_tok.wait_recv()
    copies.sent(send_tok)
    send_go.wait_recv()
    copies.sent(send_go)
    order = {"far": 0, "right": 1, "left": 2, "own": 3}

    def out_chunk(which):
        rows = pl.ds(pl.multiple_of(ring_y[which] * W, 16), W)
        cp[pl.ds(order[which] * W, W), :] = dot_t(wot[rows, :], mx[:, 0:W])

    def y_slot(buf):
        def slot(which, h):
            return buf.at[pl.ds(order[which] * W + h * (W // 2), W // 2), :]

        return slot

    up, down = along_y((y + 1) % 4), along_y((y + 3) % 4)
    ring_c = Ring(copies, down, up, y_slot(cp), cbox, W // 2)
    out_chunk("far")
    ring_c.far()

    pack_state(stb, q, [ngh, ngl],
               jnp.sum(dg[...] * q[...].astype(f32), axis=0, keepdims=True))
    state = State(stb, b0, b1, b2, bfin, bsum)
    state.step0()
    out_chunk("right")
    ring_c.near_right()
    out_chunk("left")
    ring_c.near_left()
    state.step1()

    def pack(r, one, two, rows):
        t1 = one[:, 512:WP].astype(f32)
        t2 = two[:, 512:WP].astype(f32)
        tail = t1 + pltpu.roll(t2, 48, 1)
        send[r, 0:512] = one[:, 0:512].astype(f32)
        send[r, 512:1024] = two[:, 0:512].astype(f32)
        send[r, 1024:GC] = tail
        rhs[r, 0:512] = one[:, 0:512]
        rhs[r, 512:1024] = two[:, 0:512]
        rhs[r, 1024:GC] = tail.astype(bf16)

    def query_grad(i):
        r = pl.ds(pl.multiple_of(i * 128, 128), 128)
        high, low = ngh[r, :], ngl[r, :]
        value = dot_t(high, kvh[...]) + dot_t(high, kvl[...]) + dot_t(low, kvh[...])
        value = value + dg[r, :] * ksum
        value = jnp.where(q[r, :].astype(f32) > 0, value, 0.0).astype(bf16)
        gm[r, :] = value
        pack(r, mx[r, :], value, 128)

    loop(T // 128, query_grad)
    dq = gm
    pair = copies.start(send, recv, partner)
    state.step2()

    def cast_rows(dst, base):
        def cast(i):
            r = pl.multiple_of(i * 288, 16)
            dst[pl.ds(r, 288), T:2 * T] = dp[pl.ds(pl.multiple_of(base + r, 8), 288), :].astype(bf16)

        loop(GR // 288, cast)

    cast_rows(tokt, 0)
    cast_rows(got, GR)
    out_chunk("own")
    state.step3()

    def take_pair():
        def cast(i):
            r = pl.multiple_of(i * 128, 128)
            rhs[pl.ds(T + r, 128), :] = recv[pl.ds(r, 128), :].astype(bf16)

        loop(T // 128, cast)

    pair.wait_recv()
    take_pair()
    copies.sent(pair)

    ring_f = {"far": (fa + 2) % 4, "right": (fa + 1) % 4, "left": (fa + 3) % 4, "own": fa}
    lane = functools.partial(lax.broadcasted_iota, jnp.int32, (2 * T, 128), 1)

    def place_of(which, i):
        return pl.ds(order[which] * CH + i * 144, 144) if which != "own" else pl.ds(i * 144, 144)

    def first_pair(which):
        dst = own1 if which == "own" else gbuf
        base = 0 if which == "own" else order[which] * CH

        def tile(i):
            rows = pl.ds(pl.multiple_of(ring_f[which] * CH + i * 144, 16), 144)
            to = pl.ds(pl.multiple_of(base + i * 144, 16), 144)
            lo, lt = got[rows, :], tokt[rows, :]
            tail = rhs[:, 1024:GC].astype(f32)
            tail1 = jnp.where(lane() < 48, tail, 0.0).astype(bf16)
            tail2 = jnp.where(lane() < 48, 0.0, tail).astype(bf16)
            dst[to, 0:512] = dot(lo, rhs[:, 0:512])
            dst[to, 512:1024] = dot(lt, rhs[:, 512:1024])
            dst[to, 1024:GC] = dot(lo, tail1) + dot(lt, tail2)

        loop(2, tile)

    def second_pair(which):
        dst = own2 if which == "own" else gbuf
        base = 0 if which == "own" else order[which] * CH

        def tile(i):
            rows = pl.ds(pl.multiple_of(ring_f[which] * CH + i * 144, 16), 144)
            to = pl.ds(pl.multiple_of(base + i * 144, 16), 144)
            dst[to, :] = dot(tokt[rows, :], rhs[...])

        loop(2, tile)

    def g_slot(which, h):
        return gbuf.at[pl.ds(order[which] * CH + h * 144, 144), :]

    def p_slot(buf):
        far = {"far": (sa + 2) % 4, "right": (sa + 1) % 4, "left": (sa + 3) % 4}

        def slot(which, h):
            base = far[which] * RP
            if h == 0:
                return buf.at[pl.ds(pl.multiple_of(base, 8), 40), :]
            return buf.at[pl.ds(pl.multiple_of(base + 40, 8), 32), :]

        return slot

    fr, fl = first((fa + 1) % 4), first((fa + 3) % 4)
    sr, sl = second((sa + 1) % 4), second((sa + 3) % 4)
    ring_1 = Ring(copies, fl, fr, g_slot, box1, 144)
    ring_2 = Ring(copies, fl, fr, g_slot, box2, 144)
    ring_p = Ring(copies, sl, sr, p_slot(own1), pbox1, 40)
    ring_r = Ring(copies, sl, sr, p_slot(own2), pbox2, 40)

    first_pair("far")
    ring_1.far()
    first_pair("right")
    ring_1.near_right()
    first_pair("left")
    ring_1.near_left()
    state.step4()
    ring_c.combine()
    first_pair("own")

    state.done()
    unpack_state(bfin)
    gsum = sums_row(bfin)
    dk, dv = ngh, ngl

    def key_value_grad(i):
        r = pl.ds(pl.multiple_of(i * 128, 128), 128)
        kt, vt = k[r, :], v[r, :]
        one = dot_t(vt, kvh[...]) + dot_t(vt, kvl[...]) + gsum
        one = jnp.where(kt.astype(f32) > 0, one, 0.0).astype(bf16)
        two = (dot(kt, kvh[...]) + dot(kt, kvl[...])).astype(bf16)
        dk[r, :] = one
        dv[r, :] = two
        pack(r, one, two, 128)

    loop(T // 128, key_value_grad)
    pair = copies.start(send, recv, partner)

    def in_chunk(which, place):
        def part(i, grad):
            return dot_t(wslot[place, W * i:W * i + W, :], grad[:, 0:W])

        dp[pl.ds(order[which] * W, W), :] = part(0, dq) + part(1, dk) + part(2, dv)

    ring_d = Ring(copies, down, up, y_slot(dp), dbox, W // 2)
    for copy in fetch_far:
        copy.wait()
    in_chunk("far", 0)
    ring_d.far()
    fetch_left = fetch("left", 0)
    ring_1.combine()
    for copy in fetch_right:
        copy.wait()
    in_chunk("right", 1)
    ring_d.near_right()
    fetch_own = fetch("own", 1)
    for copy in fetch_left:
        copy.wait()
    in_chunk("left", 0)
    ring_d.near_left()

    pair.wait_recv()
    take_pair()
    ring_1.sent(("a0", "a1"))
    second_pair("far")
    ring_2.far()
    second_pair("own")
    for copy in fetch_own:
        copy.wait()
    in_chunk("own", 1)

    ring_1.sent(("d0", "d1", "c0", "c1"))
    second_pair("right")
    ring_2.near_right()
    second_pair("left")
    ring_2.near_left()

    def add_up(dst, box, rows, tile):
        def step(i):
            r = pl.ds(pl.multiple_of(i * tile, 8), tile)
            dst[r, :] = dst[r, :] + (box[1, r, :] + box[2, r, :])

        loop(rows // tile, step)

    ring_1.arrived()
    add_up(own1, box1, CH, 96)
    ring_p.far()
    ring_p.near_right()
    ring_p.near_left()

    ring_c.arrived()

    def attn_sum(i):
        r = pl.multiple_of(i * 112, 8)
        at = pl.ds(pl.multiple_of(3 * W + r, 8), 112)
        rb = pl.ds(r, 112)
        cp[at, :] = cp[at, :] + (cbox[1, rb, :] + cbox[2, rb, :])

    loop(W // 112, attn_sum)
    out_c = local(cp.at[pl.ds(3 * W, W), :], at_o, out_sem.at[0])

    ring_2.combine()
    ring_p.combine()
    ring_d.combine()

    def final(src, box, out, sem):
        rows = pl.ds(pl.multiple_of(sa * RP, 8), RP)
        src[rows, :] = src[rows, :] + (box[1] + box[2])
        return local(src.at[rows, :], out, sem)

    ring_p.arrived()
    out_1 = final(own1, pbox1, g1_o, out_sem.at[1])

    ring_2.arrived()
    add_up(own2, box2, CH, 96)
    ring_r.far()
    ring_r.near_right()
    ring_r.near_left()
    ring_r.combine()
    ring_r.arrived()
    out_2 = final(own2, pbox2, g2_o, out_sem.at[2])

    ring_d.arrived()

    def tok_sum(i):
        r = pl.multiple_of(i * 112, 8)
        at = pl.ds(pl.multiple_of(3 * W + r, 8), 112)
        rb = pl.ds(r, 112)
        dp[at, :] = dp[at, :] + (dbox[1, rb, :] + dbox[2, rb, :])

    loop(W // 112, tok_sum)
    out_d = local(dp.at[pl.ds(3 * W, W), :], gt_o, out_sem.at[3])
    copies.finish()
    for copy in (out_c, out_1, out_2, out_d):
        copy.wait()


def body(tokens, w_query, w_key, w_value, w_out, grad_out):
    shapes = [
        ((T, D), bf16), ((T, D), bf16), ((2, D, W), bf16), ((W, D), bf16), ((D, W), bf16),
        ((GR, 2 * T), bf16), ((GR, 2 * T), bf16),
        ((T, WP), bf16), ((T, WP), bf16), ((T, WP), bf16), ((T, WP), bf16), ((T, WP), bf16),
        ((T, WP), bf16), ((T, WP), bf16), ((T, WP), f32),
        ((WP, WP), bf16), ((WP, WP), bf16), ((WP, WP), bf16),
        ((T, GC), f32), ((T, GC), f32), ((2 * T, GC), bf16),
        ((3 * CH, GC), f32), ((CH, GC), f32), ((CH, GC), f32),
        ((3, CH, GC), f32), ((3, CH, GC), f32), ((3, RP, GC), f32), ((3, RP, GC), f32),
        ((2 * GR, T), f32), ((2 * GR, T), f32), ((3, W, T), f32), ((3, W, T), f32),
    ]
    for _ in range(2):
        shapes += [((SR, 128), f32), ((SR // 2, 128), f32), ((3, RP, 128), f32), ((3, RP, 128), f32),
                   ((SR, 128), f32), ((RP, 128), f32)]
    scratch = [pltpu.VMEM(*shape) for shape in shapes]
    scratch += [
        pltpu.SemaphoreType.DMA((6,)), pltpu.SemaphoreType.DMA((2, 3)), pltpu.SemaphoreType.DMA((4,)),
        pltpu.SemaphoreType.DMA((64,)), pltpu.SemaphoreType.DMA((64,)),
    ]
    at, gt, g1, g2 = pl.pallas_call(
        kernel,
        out_shape=(
            jax.ShapeDtypeStruct((W, T), f32), jax.ShapeDtypeStruct((W, T), f32),
            jax.ShapeDtypeStruct((RP, GC), f32), jax.ShapeDtypeStruct((RP, GC), f32),
        ),
        in_specs=[pl.BlockSpec(memory_space=pl.ANY)] * 6,
        out_specs=[pl.BlockSpec(memory_space=pl.ANY)] * 4,
        scratch_shapes=scratch,
        compiler_params=pltpu.CompilerParams(
            collective_id=0, has_side_effects=True, vmem_limit_bytes=64 * 1024 * 1024 - 65536),
        cost_estimate=pl.CostEstimate(flops=16 * 10**9, bytes_accessed=16 * 10**6, transcendentals=0),
        name="fused_attention",
    )(tokens, w_query, w_key, w_value, w_out, grad_out)
    factor = 1.0 / math.sqrt(T * lax.axis_size("seq"))
    g1 = g1[:ROWS] * factor
    g2 = g2[:ROWS] * factor

    def one(g):
        return jnp.concatenate([g[:, 0:512], g[:, 1024:1072]], axis=1)

    def two(g):
        return jnp.concatenate([g[:, 512:1024], g[:, 1072:1120]], axis=1)

    return (at.T.astype(bf16), gt.T.astype(bf16), two(g1), one(g2), two(g2), one(g1).T)


def solution(mesh):
    in_specs = (
        P("seq", None),
        P(None, "head"),
        P(None, "head"),
        P(None, "head"),
        P("head", None),
        P("seq", None),
    )
    out_specs = (
        P("seq", "head"),
        P("seq", "head"),
        P("seq", "head"),
        P("seq", "head"),
        P("seq", "head"),
        P("head", "seq"),
    )
    return jax.shard_map(body, mesh=mesh, in_specs=in_specs, out_specs=out_specs, check_vma=False)
```

time: 506 us -> 131 us (0.26)
  blocking collectives: 221 us -> 0 us
  waiting for transfers between devices: 201 us -> 0 us
  Pallas kernels: 0 us -> 106 us
  matrix products: 46.6 us -> 0 us
  between operations: 15.3 us -> 0.68 us
  local copies, waits for them, and re-layouts: 8 us -> 18.5 us
  starting transfers between devices: 5.37 us -> 0 us
    psum x2 -> x0, blocking collectives: 135 us -> none  [the longest x1 68.4 us: body(): kv_state, key_sum = lax.psum((state_part, ksum_part), 'seq')]
    pallas_call x0 -> x1, Pallas kernels: none -> 106 us  [body(): pl.pallas_call(kernel, out_shape=(jax.ShapeDtypeStruct((W, T), f32), jax....]
    unnamed x9 -> x0, waiting for transfers between devices: 103 us -> none
    psum x1 -> x0, waiting for transfers between devices: 98.6 us -> none  [body(): kv_state, key_sum = lax.psum((state_part, ksum_part), 'seq')]
    unnamed x1 -> x0, blocking collectives: 85.8 us -> none
    dot_general x18 -> x0, matrix products: 46.6 us -> none  [the longest x1 9.14 us: body(): jnp.einsum('tr,tc->rc', tokens, stacked, preferred_element_type=f32)]
    unnamed x42 -> x13, local copies, waits for them, and re-layouts: 7.86 us -> 18.3 us
    unnamed x5 -> x0, starting transfers between devices: 5.25 us -> none
  transfers between devices with their start and end apart: 8 -> 0, of which waited for: 3 -> 0; matrix products, arithmetic and copies ran while one was open for 24% -> 0% of each run, Pallas kernels for 0% -> 0%
where the time goes in v1:
time: 131 us
  Pallas kernels  106 us (81%)
  local copies, waits for them, and re-layouts  18.5 us (14%)
  other arithmetic  5.29 us (4%)
    pallas_call x1, Pallas kernels, body(): pl.pallas_call(kernel, out_shape=(jax.ShapeDtypeStruct((W, T), f32), jax....  106 us
    unnamed x13, local copies, waits for them, and re-layouts  18.3 us

profile of v1, /device:TPU:0, one launch (start us, length us, event | category | flops | bytes accessed | tf_op | source)
XLA Modules:
  0.0 130.8 jit_solution(7156782957939296661)
XLA Ops:
  0.6 3.8 %copy.12.tok_h = bf16[384,2240]{1,0:T(8,128)(2,1)} copy(bf16[384,2240]{0,1:T(8,128)(2,1)} %param.6) | data formatting | bytes 3440640 | tf_op args[0]
  4.4 0.0 copy-start
  4.4 4.0 %copy.16.go_h = bf16[384,2240]{1,0:T(8,128)(2,1)} copy(bf16[384,2240]{0,1:T(8,128)(2,1)} %param.11) | data formatting | bytes 3440640 | tf_op args[5]
  8.4 0.0 copy-done
  8.4 2.9 %copy.13.wq_h = bf16[2240,560]{1,0:T(8,128)(2,1)} copy(bf16[2240,560]{0,1:T(8,128)(2,1)S(1)} %copy-done) | data formatting | bytes 5017600 | tf_op args[1]
  11.3 0.0 copy-start.1
  11.3 4.7 %copy.14.wk_h = bf16[2240,560]{1,0:T(8,128)(2,1)} copy(bf16[2240,560]{0,1:T(8,128)(2,1)} %param.8) | data formatting | bytes 5017600 | tf_op args[2]
  16.0 0.0 copy-done.1
  16.0 2.9 %copy.15.wv_h = bf16[2240,560]{1,0:T(8,128)(2,1)} copy(bf16[2240,560]{0,1:T(8,128)(2,1)S(1)} %copy-done.1) | data formatting | bytes 5017600 | tf_op args[3]
  18.9 106.3 %fused_attention.1 = (f32[560,384]{1,0:T(8,128)}, f32[560,384]{1,0:T(8,128)}, f32[72,1152]{1,0:T(8,128)}, f32[72,1152]{1,0:T(8,128)}) custom-call(bf16[384,2240]{1,0:T(8,128)(2,1)} %copy.12.tok_h, bf16[2240,560]{1,0:T(8,128)(2,1)} %copy.13.wq_h, bf16[2240,560]{1,0:T(8,128)(2,1)} %copy.14.wk_h, bf16[2240,560]{1,0:T(8,128)(2,1)} %copy.15.wv_h, ...), custom_call_target="tpu_custom_call" | custom-call | flops 16000000000 | bytes 16000000 | tf_op jit(solution)/shard_map/fused_attention/pallas_call | solution.py:646
  125.2 0.0 copy-start.2
  125.2 0.0 copy-start.3
  125.2 2.5 %convert_bitcast_fusion = (bf16[384,560]{0,1:T(8,128)(2,1)}, bf16[384,560]{0,1:T(8,128)(2,1)}) fusion(f32[560,384]{1,0:T(8,128)} %get-tuple-element.11, f32[560,384]{1,0:T(8,128)} %get-tuple-element.10), kind=kLoop, calls=%fused_computation | loop fusion | flops 430080 | bytes 2580480 | tf_op jit(solution)/shard_map/convert_element_type | solution.py:670
  127.7 0.0 copy-done.2
  127.7 0.0 copy-done.3
  127.7 0.1 slice_multiply_fusion
  127.8 0.1 fusion.3
  127.9 0.7 pad_maximum_fusion.2
  128.6 0.7 pad_maximum_fusion.1
  129.3 0.1 fusion.1
  129.4 0.7 maximum_bitcast_fusion
  130.1 0.7 pad_maximum_fusion
  (2 shorter events, 0.1 us)
Async XLA Ops:
  4.4 4.0 %copy-start = (bf16[2240,560]{0,1:T(8,128)(2,1)S(1)}, bf16[2240,560]{0,1:T(8,128)(2,1)}, u32[]{:S(2)}) copy-start(bf16[2240,560]{0,1:T(8,128)(2,1)} %param.7) | copy-start | bytes 7526404
  11.3 4.7 %copy-start.1 = (bf16[2240,560]{0,1:T(8,128)(2,1)S(1)}, bf16[2240,560]{0,1:T(8,128)(2,1)}, u32[]{:S(2)}) copy-start(bf16[2240,560]{0,1:T(8,128)(2,1)} %param.9) | copy-start | bytes 7526404
  125.2 2.5 %copy-start.2 = (f32[72,1152]{1,0:T(8,128)S(1)}, f32[72,1152]{1,0:T(8,128)}, u32[]{:S(2)}) copy-start(f32[72,1152]{1,0:T(8,128)} %get-tuple-element.12) | copy-start | bytes 995332
  125.2 2.5 %copy-start.3 = (f32[72,1152]{1,0:T(8,128)S(1)}, f32[72,1152]{1,0:T(8,128)}, u32[]{:S(2)}) copy-start(f32[72,1152]{1,0:T(8,128)} %get-tuple-element.13) | copy-start | bytes 995332

commit v2 on v1

v2 whole, which is shorter than its diff:
```python
import functools
import math

import jax
import jax.numpy as jnp
from jax import lax
from jax.experimental import pallas as pl
from jax.experimental.pallas import tpu as pltpu
from jax.sharding import PartitionSpec as P

f32 = jnp.float32
bf16 = jnp.bfloat16
MESH = pl.DeviceIdType.MESH

D = 2240
W = 560
HEADS = 5
HP = 128
T = 384
HD = 112
ROWS = 70
RP = 72
NB = 16
GR = NB * RP
GC = 1152
CH = 4 * RP
SR = 576
EPS = 1e-15


def dot(a, b):
    return lax.dot_general(a, b, (((1,), (0,)), ((), ())), preferred_element_type=f32)


def dot_t(a, b):
    return lax.dot_general(a, b, (((1,), (1,)), ((), ())), preferred_element_type=f32)


def dot_n(a, b):
    return lax.dot_general(a, b, (((0,), (0,)), ((), ())), preferred_element_type=f32)


def parts(v):
    high = v.astype(bf16)
    return high, (v - high.astype(f32)).astype(bf16)


def loop(count, fn):
    def step(i, carry):
        fn(i)
        return carry

    lax.fori_loop(0, count, step, 0)


class Copies:
    def __init__(self, send, recv):
        self.send, self.recv, self.used, self.open = send, recv, 0, []

    def start(self, src, dst, device):
        k = self.used
        self.used += 1
        copy = pltpu.make_async_remote_copy(
            src_ref=src, dst_ref=dst, send_sem=self.send.at[k], recv_sem=self.recv.at[k],
            device_id=device, device_id_type=MESH)
        copy.start()
        self.open.append(copy)
        return copy

    def sent(self, copy):
        copy.wait_send()
        self.open = [other for other in self.open if other is not copy]

    def finish(self):
        for copy in self.open:
            copy.wait_send()
        self.open = []


class Ring:
    def __init__(self, copies, left, right, slot, box, cut):
        self.copies, self.left, self.right, self.slot = copies, left, right, slot
        self.box, self.cut = box, cut
        self.rows = box.shape[1]

    def land(self, kind, half):
        if half == 0:
            return self.box.at[kind, pl.ds(0, self.cut), :]
        return self.box.at[kind, pl.ds(self.cut, self.rows - self.cut), :]

    def far(self):
        self.a0 = self.copies.start(self.slot("far", 0), self.land(0, 0), self.right)
        self.a1 = self.copies.start(self.slot("far", 1), self.land(0, 1), self.left)

    def near_right(self):
        self.d1 = self.copies.start(self.slot("right", 1), self.land(1, 1), self.right)

    def near_left(self):
        self.d0 = self.copies.start(self.slot("left", 0), self.land(1, 0), self.left)

    def combine(self):
        self.a0.wait_recv()
        ref = self.slot("right", 0)
        ref[...] = ref[...] + self.land(0, 0)[...]
        self.c0 = self.copies.start(ref, self.land(2, 0), self.right)
        self.a1.wait_recv()
        ref = self.slot("left", 1)
        ref[...] = ref[...] + self.land(0, 1)[...]
        self.c1 = self.copies.start(ref, self.land(2, 1), self.left)

    def arrived(self):
        for copy in (self.d0, self.d1, self.c0, self.c1):
            copy.wait_recv()

    def sent(self, names):
        for name in names:
            self.copies.sent(getattr(self, name))


def kernel(tok_h, wq_h, wk_h, wv_h, wo_h, go_h,
           at_o, gt_o, g1_o, g2_o,
           tok, go, wslot, wot, wqn, wkn, wvn, tokt, got,
           q, k, v, gm, ngh, ngl, rhs1, rhs2, send, recv,
           gbuf, own1, own2, box1, box2, pbox1, pbox2,
           cp, dp, cbox, dbox,
           sta, a0, a1, a2, afin, asum, stb, b0, b1, b2, bfin, bsum,
           in_sem, out_sem, ssem, rsem):
    s = lax.axis_index("seq")
    y = lax.axis_index("head")
    c = s % 2
    chip = s // 2
    x = chip // 4
    z = chip % 4
    fa = x * (1 - c) + z * c
    sa = z * (1 - c) + x * c

    def first(i):
        return {"seq": ((i * (1 - c) + sa * c) * 4 + sa * (1 - c) + i * c) * 2 + c, "head": y}

    def second(i):
        return {"seq": ((fa * (1 - c) + i * c) * 4 + i * (1 - c) + fa * c) * 2 + c, "head": y}

    def along_y(i):
        return {"seq": s, "head": i}

    partner = {"seq": s + 1 - 2 * c, "head": y}

    def local(src, dst, sem):
        copy = pltpu.make_async_copy(src, dst, sem)
        copy.start()
        return copy

    in_tok = local(tok_h, tok, in_sem.at[0])
    in_k = local(wk_h, wslot.at[0], in_sem.at[1])
    in_v = local(wv_h, wslot.at[1], in_sem.at[2])
    in_go = local(go_h, go, in_sem.at[3])

    barrier = pltpu.get_barrier_semaphore()
    peers = [partner, along_y((y + 1) % 4), along_y((y + 3) % 4)]
    peers += [first((fa + d) % 4) for d in (1, 2, 3)]
    peers += [second((sa + d) % 4) for d in (1, 2, 3)]
    for peer in peers:
        pl.semaphore_signal(barrier, inc=1, device_id=peer, device_id_type=MESH)

    copies = Copies(ssem, rsem)

    def head(h):
        return pl.ds(pl.multiple_of(h * HD, 16), HD)

    def block(h):
        return pl.ds(pl.multiple_of(h * HP, HP), HP)

    def sum_row(row):
        keep = lax.broadcasted_iota(jnp.int32, (HP - HD, T), 0) == 0
        return jnp.where(keep, row, 0.0)

    def state_part(st, left, rights):
        def one(h):
            total = None
            for right in rights:
                value = dot_t(left[head(h), :], right[block(h), :])
                total = value if total is None else total + value
            st[head(h), :] = total

        loop(HEADS, one)
        st[W:SR, :] = jnp.zeros((SR - W, HP), f32)

    half = SR // 2
    piece = half // 4
    mine = pl.multiple_of(c * half, 8)
    other = pl.multiple_of((1 - c) * half, 8)

    def mine_piece(i):
        return pl.ds(pl.multiple_of(c * half + i * piece, 8), piece)

    class State:
        def __init__(self, st, r0, r1, r2, fin, total):
            self.st, self.r0, self.r1, self.r2, self.fin, self.total = st, r0, r1, r2, fin, total

        def step0(self):
            self.c = copies.start(self.st.at[pl.ds(other, half), :], self.r0, partner)

        def step1(self):
            self.c.wait_recv()
            rows = pl.ds(mine, half)
            self.st[rows, :] = self.st[rows, :] + self.r0[...]
            self.cs = [copies.start(self.st.at[mine_piece((fa + d) % 4), :], self.r1.at[d - 1],
                                    first((fa + d) % 4)) for d in (1, 2, 3)]

        def step2(self):
            for copy in self.cs:
                copy.wait_recv()
            self.total[...] = (self.st[mine_piece(fa), :] + self.r1[0]) + (self.r1[1] + self.r1[2])
            self.cs = [copies.start(self.total, self.r2.at[d - 1], second((sa + d) % 4))
                       for d in (1, 2, 3)]

        def step3(self):
            for copy in self.cs:
                copy.wait_recv()
            rows = mine_piece(fa)
            self.fin[rows, :] = (self.total[...] + self.r2[0]) + (self.r2[1] + self.r2[2])
            self.cs = [copies.start(self.fin.at[rows, :], self.fin.at[rows, :], first((fa + d) % 4))
                       for d in (1, 2, 3)]

        def step4(self):
            for copy in self.cs:
                copy.wait_recv()
            rows = pl.ds(mine, half)
            self.c = copies.start(self.fin.at[rows, :], self.fin.at[rows, :], partner)

        def done(self):
            self.c.wait_recv()

    in_tok.wait()
    in_k.wait()
    k[...] = jnp.maximum(dot(wslot[0], tok[...]), 0.0).astype(bf16)
    in_q = local(wq_h, wslot.at[0], in_sem.at[4])
    in_v.wait()
    value = dot(wslot[1], tok[...]).astype(bf16)
    for h in range(HEADS):
        v[HP * h:HP * h + HD, :] = value[HD * h:HD * h + HD, :]
        v[HP * h + HD:HP * h + HP, :] = sum_row(jnp.ones((1, T), f32)).astype(bf16)
    in_o = local(wo_h, wslot.at[1], in_sem.at[5])
    state_part(sta, k, [v])
    pl.semaphore_wait(barrier, len(peers))
    state = State(sta, a0, a1, a2, afin, asum)
    state.step0()

    in_q.wait()
    q[...] = jnp.maximum(dot(wslot[0], tok[...]), 0.0).astype(bf16)
    state.step1()

    def gather_rows(src, base, which):
        for b in range(NB):
            lo = 2 * ROWS * b
            w0 = lo // 16 * 16
            w1 = -(-(lo + 2 * ROWS) // 16) * 16
            i = lax.broadcasted_iota(jnp.int32, (RP, w1 - w0), 0)
            j = lax.broadcasted_iota(jnp.int32, (RP, w1 - w0), 1)
            pick = jnp.logical_and(j == i + (lo - w0) + ROWS * which, i < ROWS)
            place = b * (1 - which) + (b % 4 * 4 + b // 4) * which
            cp[pl.ds(pl.multiple_of(base + place * RP, 8), RP), :] = dot(
                pick.astype(f32).astype(bf16), src[w0:w1, :])

    def rows_of(src, dst, base):
        gather_rows(src, base, c)

        def cast(i):
            r = pl.multiple_of(i * 288, 16)
            dst[pl.ds(r, 288), 0:T] = cp[pl.ds(pl.multiple_of(base + r, 8), 288), :].astype(bf16)

        loop(GR // 288, cast)
        gather_rows(src, base, 1 - c)
        place = pl.ds(base, GR)
        return copies.start(cp.at[place, :], dp.at[place, :], partner)

    def flip(src, dst):
        def columns(start, n):
            eye = (lax.broadcasted_iota(jnp.int32, (n, n), 0) == lax.broadcasted_iota(jnp.int32, (n, n), 1))
            dst[pl.ds(start, n), :] = dot_t(
                eye.astype(f32).astype(bf16), src[:, pl.ds(start, n)]).astype(bf16)

        loop(D // 256, lambda i: columns(pl.multiple_of(i * 256, 256), 256))
        columns(D // 256 * 256, D % 256)

    send_tok = rows_of(tok, tokt, 0)
    state.step2()

    in_o.wait()
    in_go.wait()
    gm[...] = dot(wslot[1], go[...]).astype(bf16)
    state.step3()
    send_go = rows_of(go, got, GR)
    state.step4()
    flip(wslot.at[1], wot)
    in_v = local(wv_h, wslot.at[1], in_sem.at[2])
    rhs1[2 * W:GC, :] = jnp.zeros((GC - 2 * W, 2 * T), bf16)
    rhs2[2 * W:GC, :] = jnp.zeros((GC - 2 * W, 2 * T), bf16)

    state.done()

    def attend(h):
        high, low = parts(afin[head(h), :])
        qt = q[head(h), :]
        both = dot_n(high, qt) + dot_n(low, qt)
        rec = 1.0 / (both[HD:HD + 1, :] + EPS)
        att = both[0:HD, :] * rec
        rhs1[head(h), 0:T] = att.astype(bf16)
        send[head(h), :] = att.astype(bf16).astype(f32)
        g = gm[head(h), :].astype(f32)
        grad = -jnp.sum(g * att, axis=0, keepdims=True) * rec
        high, low = parts(g * rec)
        at = pl.ds(pl.multiple_of(h * HP, HP), HD)
        ngh[at, :] = high
        ngl[at, :] = low
        high, low = parts(sum_row(grad))
        at = pl.ds(pl.multiple_of(h * HP + HD, 16), HP - HD)
        ngh[at, :] = high
        ngl[at, :] = low

    loop(HEADS, attend)

    ring_y = {"far": (y + 2) % 4, "right": (y + 1) % 4, "left": (y + 3) % 4, "own": y}
    order = {"far": 0, "right": 1, "left": 2, "own": 3}
    copies.sent(send_tok)
    copies.sent(send_go)

    def y_rows(which):
        return pl.ds(pl.multiple_of(ring_y[which] * W, 16), W)

    def out_chunk(which):
        cp[pl.ds(order[which] * W, W), :] = dot(wot[y_rows(which), :], rhs1[0:W, 0:T])

    def y_slot(buf):
        def slot(which, h):
            return buf.at[pl.ds(order[which] * W + h * (W // 2), W // 2), :]

        return slot

    up, down = along_y((y + 1) % 4), along_y((y + 3) % 4)
    ring_c = Ring(copies, down, up, y_slot(cp), cbox, W // 2)
    out_chunk("far")
    ring_c.far()

    state_part(stb, q, [ngh, ngl])
    state = State(stb, b0, b1, b2, bfin, bsum)
    state.step0()
    out_chunk("right")
    ring_c.near_right()
    out_chunk("left")
    ring_c.near_left()
    state.step1()

    def query_grad(h):
        high, low = parts(afin[head(h), :])
        ng = ngh[block(h), :]
        value = dot(high, ng) + dot(low, ng) + dot(high, ngl[block(h), :])
        value = jnp.where(q[head(h), :].astype(f32) > 0, value, 0.0).astype(bf16)
        at = pl.ds(pl.multiple_of(W + h * HD, 16), HD)
        rhs1[at, 0:T] = value
        send[at, :] = value.astype(f32)

    loop(HEADS, query_grad)
    pair = copies.start(send, recv, partner)
    state.step2()

    def cast_rows(dst, base):
        def cast(i):
            r = pl.multiple_of(i * 288, 16)
            dst[pl.ds(r, 288), T:2 * T] = dp[pl.ds(pl.multiple_of(base + r, 8), 288), :].astype(bf16)

        loop(GR // 288, cast)

    flip(wslot.at[0], wqn)
    in_k = local(wk_h, wslot.at[0], in_sem.at[1])
    send_tok.wait_recv()
    cast_rows(tokt, 0)
    send_go.wait_recv()
    cast_rows(got, GR)
    state.step3()

    def take_pair(dst):
        def cast(i):
            r = pl.ds(pl.multiple_of(i * HD, 16), HD)
            dst[r, T:2 * T] = recv[r, :].astype(bf16)

        loop(2 * W // HD, cast)

    pair.wait_recv()
    take_pair(rhs1)
    copies.sent(pair)

    ring_f = {"far": (fa + 2) % 4, "right": (fa + 1) % 4, "left": (fa + 3) % 4, "own": fa}

    def tiles_of(which, dst, fn):
        base = 0 if which == "own" else order[which] * CH

        def tile(i):
            rows = pl.ds(pl.multiple_of(ring_f[which] * CH + i * 144, 16), 144)
            fn(rows, dst, pl.ds(pl.multiple_of(base + i * 144, 16), 144))

        loop(2, tile)

    def first_tile(rows, dst, to):
        lo, lt = got[rows, :], tokt[rows, :]
        dst[to, 0:512] = dot_t(lo, rhs1[0:512, :])
        shared = rhs1[512:640, :]
        is_out = lax.broadcasted_iota(jnp.int32, (144, 128), 1) < W - 512
        dst[to, 512:640] = jnp.where(is_out, dot_t(lo, shared), dot_t(lt, shared))
        dst[to, 640:GC] = dot_t(lt, rhs1[640:GC, :])

    def second_tile(rows, dst, to):
        dst[to, :] = dot_t(tokt[rows, :], rhs2[...])

    def first_pair(which):
        tiles_of(which, own1 if which == "own" else gbuf, first_tile)

    def second_pair(which):
        tiles_of(which, own2 if which == "own" else gbuf, second_tile)

    def g_slot(which, h):
        return gbuf.at[pl.ds(order[which] * CH + h * 144, 144), :]

    def p_slot(buf):
        far = {"far": (sa + 2) % 4, "right": (sa + 1) % 4, "left": (sa + 3) % 4}

        def slot(which, h):
            base = far[which] * RP
            if h == 0:
                return buf.at[pl.ds(pl.multiple_of(base, 8), 40), :]
            return buf.at[pl.ds(pl.multiple_of(base + 40, 8), 32), :]

        return slot

    fr, fl = first((fa + 1) % 4), first((fa + 3) % 4)
    sr, sl = second((sa + 1) % 4), second((sa + 3) % 4)
    ring_1 = Ring(copies, fl, fr, g_slot, box1, 144)
    ring_2 = Ring(copies, fl, fr, g_slot, box2, 144)
    ring_p = Ring(copies, sl, sr, p_slot(own1), pbox1, 40)
    ring_r = Ring(copies, sl, sr, p_slot(own2), pbox2, 40)

    first_pair("far")
    ring_1.far()
    state.step4()
    first_pair("right")
    ring_1.near_right()
    first_pair("left")
    ring_1.near_left()
    ring_c.combine()
    in_v.wait()
    flip(wslot.at[1], wvn)
    in_k.wait()
    flip(wslot.at[0], wkn)

    state.done()

    def key_value_grad(h):
        high, low = parts(bfin[head(h), :])
        kt, vt = k[head(h), :], v[block(h), :]
        one = dot(high, vt) + dot(low, vt)
        one = jnp.where(kt.astype(f32) > 0, one, 0.0).astype(bf16)
        two = (dot_n(high, kt) + dot_n(low, kt))[0:HD, :].astype(bf16)
        rhs2[head(h), 0:T] = one
        send[head(h), :] = one.astype(f32)
        at = pl.ds(pl.multiple_of(W + h * HD, 16), HD)
        rhs2[at, 0:T] = two
        send[at, :] = two.astype(f32)

    loop(HEADS, key_value_grad)
    pair = copies.start(send, recv, partner)

    def in_chunk(which):
        rows = y_rows(which)
        dp[pl.ds(order[which] * W, W), :] = (
            dot(wqn[rows, :], rhs1[W:2 * W, 0:T]) + dot(wkn[rows, :], rhs2[0:W, 0:T])
            + dot(wvn[rows, :], rhs2[W:2 * W, 0:T]))

    ring_d = Ring(copies, down, up, y_slot(dp), dbox, W // 2)
    in_chunk("far")
    ring_d.far()
    ring_1.combine()
    in_chunk("right")
    ring_d.near_right()
    in_chunk("left")
    ring_d.near_left()

    pair.wait_recv()
    take_pair(rhs2)
    first_pair("own")
    ring_1.sent(("a0", "a1"))
    second_pair("far")
    ring_2.far()
    second_pair("own")
    out_chunk("own")
    in_chunk("own")

    ring_1.sent(("d0", "d1", "c0", "c1"))
    second_pair("right")
    ring_2.near_right()
    second_pair("left")
    ring_2.near_left()

    def add_up(dst, box, rows, tile):
        def step(i):
            r = pl.ds(pl.multiple_of(i * tile, 8), tile)
            dst[r, :] = dst[r, :] + (box[1, r, :] + box[2, r, :])

        loop(rows // tile, step)

    ring_1.arrived()
    add_up(own1, box1, CH, 96)
    ring_p.far()
    ring_p.near_right()
    ring_p.near_left()

    def y_sum(buf, box, dst, out, sem):
        def step(i):
            at = pl.ds(pl.multiple_of(3 * W + i * HD, 16), HD)
            rb = pl.ds(pl.multiple_of(i * HD, 16), HD)
            dst[rb, :] = (buf[at, :] + (box[1, rb, :] + box[2, rb, :])).astype(bf16)

        loop(HEADS, step)
        return local(dst, out, sem)

    ring_c.arrived()
    out_c = y_sum(cp, cbox, q, at_o, out_sem.at[0])

    ring_2.combine()
    ring_p.combine()
    ring_d.combine()

    def final(src, box, out, sem):
        rows = pl.ds(pl.multiple_of(sa * RP, 8), RP)
        src[rows, :] = src[rows, :] + (box[1] + box[2])
        return local(src.at[rows, :], out, sem)

    ring_p.arrived()
    out_1 = final(own1, pbox1, g1_o, out_sem.at[1])

    ring_2.arrived()
    add_up(own2, box2, CH, 96)
    ring_r.far()
    ring_r.near_right()
    ring_r.near_left()
    ring_r.combine()
    ring_r.arrived()
    out_2 = final(own2, pbox2, g2_o, out_sem.at[2])

    ring_d.arrived()
    out_d = y_sum(dp, dbox, gm, gt_o, out_sem.at[3])
    copies.finish()
    for copy in (out_c, out_1, out_2, out_d):
        copy.wait()


def finish(factor, at, gt, g1, g2, at_o, gt_o, gq_o, gk_o, gv_o, gw_o, sem):
    copies = [pltpu.make_async_copy(at, at_o, sem.at[0]), pltpu.make_async_copy(gt, gt_o, sem.at[1])]
    for copy in copies:
        copy.start()
    one, two = g1[0:ROWS, :] * factor, g2[0:ROWS, :] * factor
    gw_o[...] = one[:, 0:W]
    gq_o[...] = one[:, W:2 * W]
    gk_o[...] = two[:, 0:W]
    gv_o[...] = two[:, W:2 * W]
    for copy in copies:
        copy.wait()


def body(tokens, w_query, w_key, w_value, w_out, grad_out):
    shapes = [
        ((D, T), bf16), ((D, T), bf16), ((2, W, D), bf16),
        ((D, W), bf16), ((D, W), bf16), ((D, W), bf16), ((D, W), bf16),
        ((GR, 2 * T), bf16), ((GR, 2 * T), bf16),
        ((W, T), bf16), ((W, T), bf16), ((HEADS * HP, T), bf16), ((W, T), bf16),
        ((HEADS * HP, T), bf16), ((HEADS * HP, T), bf16),
        ((GC, 2 * T), bf16), ((GC, 2 * T), bf16), ((2 * W, T), f32), ((2 * W, T), f32),
        ((3 * CH, GC), f32), ((CH, GC), f32), ((CH, GC), f32),
        ((3, CH, GC), f32), ((3, CH, GC), f32), ((3, RP, GC), f32), ((3, RP, GC), f32),
        ((2 * GR, T), f32), ((2 * GR, T), f32), ((3, W, T), f32), ((3, W, T), f32),
    ]
    for _ in range(2):
        shapes += [((SR, HP), f32), ((SR // 2, HP), f32), ((3, RP, HP), f32), ((3, RP, HP), f32),
                   ((SR, HP), f32), ((RP, HP), f32)]
    scratch = [pltpu.VMEM(*shape) for shape in shapes]
    scratch += [
        pltpu.SemaphoreType.DMA((6,)), pltpu.SemaphoreType.DMA((4,)),
        pltpu.SemaphoreType.DMA((64,)), pltpu.SemaphoreType.DMA((64,)),
    ]
    spaces = [pl.BlockSpec(memory_space=pl.ANY)] * 6
    at, gt, g1, g2 = pl.pallas_call(
        kernel,
        out_shape=(
            jax.ShapeDtypeStruct((W, T), bf16), jax.ShapeDtypeStruct((W, T), bf16),
            jax.ShapeDtypeStruct((RP, GC), f32), jax.ShapeDtypeStruct((RP, GC), f32),
        ),
        in_specs=spaces,
        out_specs=spaces[:4],
        scratch_shapes=scratch,
        compiler_params=pltpu.CompilerParams(
            collective_id=0, has_side_effects=True, vmem_limit_bytes=64 * 1024 * 1024 - 65536),
        cost_estimate=pl.CostEstimate(flops=16 * 10**9, bytes_accessed=16 * 10**6, transcendentals=0),
        name="fused_attention",
    )(tokens.T, w_query.T, w_key.T, w_value.T, w_out, grad_out.T)
    factor = 1.0 / math.sqrt(T * lax.axis_size("seq"))
    grad = jax.ShapeDtypeStruct((ROWS, W), f32)
    vmem = pl.BlockSpec(memory_space=pltpu.VMEM)
    at, gt, gq, gk, gv, gw = pl.pallas_call(
        functools.partial(finish, factor),
        out_shape=(
            jax.ShapeDtypeStruct((W, T), bf16), jax.ShapeDtypeStruct((W, T), bf16),
            grad, grad, grad, grad,
        ),
        in_specs=spaces[:2] + [vmem] * 2,
        out_specs=spaces[:2] + [vmem] * 4,
        scratch_shapes=[pltpu.SemaphoreType.DMA((2,))],
        name="final_arrays",
    )(at, gt, g1, g2)
    return (at.T, gt.T, gq, gk, gv, gw.T)


def solution(mesh):
    in_specs = (
        P("seq", None),
        P(None, "head"),
        P(None, "head"),
        P(None, "head"),
        P("head", None),
        P("seq", None),
    )
    out_specs = (
        P("seq", "head"),
        P("seq", "head"),
        P("seq", "head"),
        P("seq", "head"),
        P("seq", "head"),
        P("head", "seq"),
    )
    return jax.shard_map(body, mesh=mesh, in_specs=in_specs, out_specs=out_specs, check_vma=False)
```

time: 131 us -> 134 us (1.023)
  Pallas kernels: 106 us -> 133 us
  local copies, waits for them, and re-layouts: 18.5 us -> 0 us
  other arithmetic: 5.29 us -> 0 us
    pallas_call x1 -> x2, Pallas kernels: 106 us -> 133 us  [the longest x1 103 us: body(): pl.pallas_call(kernel, out_shape=(jax.ShapeDtypeStruct((W, T), bf16), jax...]
    unnamed x13 -> x0, local copies, waits for them, and re-layouts: 18.3 us -> none
    convert_element_type x1 -> x0, other arithmetic: 2.48 us -> none  [body(): gt.T.astype(bf16)]
    concatenate x3 -> x0, other arithmetic: 2.06 us -> none  [the longest x2 1.38 us: two(): return jnp.concatenate([g[:, 512:1024], g[:, 1072:1120]], axis=1)]
where the time goes in v2:
time: 134 us; the launch traced here: 133 us
  Pallas kernels  133 us (99%)
    pallas_call x1, Pallas kernels, body(): pl.pallas_call(kernel, out_shape=(jax.ShapeDtypeStruct((W, T), bf16), jax...  103 us
    pallas_call x1, Pallas kernels, body(): pl.pallas_call(functools.partial(finish, factor), out_shape=(jax.ShapeDty...  29.1 us

profile of v2, /device:TPU:0, one launch (start us, length us, event | category | flops | bytes accessed | tf_op | source)
XLA Modules:
  0.0 133.4 jit_solution(7309682217569677379)
XLA Ops:
  0.6 103.5 %fused_attention.1 = (bf16[560,384]{1,0:T(8,128)(2,1)}, bf16[560,384]{1,0:T(8,128)(2,1)}, f32[72,1152]{1,0:T(8,128)}, f32[72,1152]{1,0:T(8,128)}) custom-call(bf16[2240,384]{1,0:T(8,128)(2,1)} %bitcast.11, bf16[560,2240]{1,0:T(8,128)(2,1)} %bitcast.8, bf16[560,2240]{1,0:T(8,128)(2,1)} %bitcast.9, bf16[560,2240]{1,0:T(8,128)(2,1)} %bitcast.10, ...), custom_call_target="tpu_custom_call" | custom-call | flops 16000000000 | bytes 16000000 | tf_op jit(solution)/shard_map/fused_attention/pallas_call | solution.py:590
  104.1 29.1 %final_arrays.1 = (bf16[560,384]{1,0:T(8,128)(2,1)}, bf16[560,384]{1,0:T(8,128)(2,1)}, f32[70,560]{1,0:T(8,128)}, f32[70,560]{1,0:T(8,128)}, f32[70,560]{1,0:T(8,128)}, /*index=5*/f32[70,560]{1,0:T(8,128)}) custom-call(bf16[560,384]{1,0:T(8,128)(2,1)} %get-tuple-element.16.at, bf16[560,384]{1,0:T(8,128)(2,1)} %get-tuple-element.17.gt, ...), custom_call_target="tpu_custom_call" | custom-call | tf_op jit(solution)/shard_map/final_arrays/pallas_call | solution.py:607

commit v3 on v2

--- a/solution.py
+++ b/solution.py
@@ -24,7 +24,8 @@
 GR = NB * RP
 GC = 1152
 CH = 4 * RP
-SR = 576
+PR = 24
+SR = 2 * NB * PR
 EPS = 1e-15
 
 
@@ -43,6 +44,11 @@
 def parts(v):
     high = v.astype(bf16)
     return high, (v - high.astype(f32)).astype(bf16)
+
+
+def each(count, fn):
+    for i in range(count):
+        fn(i)
 
 
 def loop(count, fn):
@@ -123,7 +129,7 @@
            q, k, v, gm, ngh, ngl, rhs1, rhs2, send, recv,
            gbuf, own1, own2, box1, box2, pbox1, pbox2,
            cp, dp, cbox, dbox,
-           sta, a0, a1, a2, afin, asum, stb, b0, b1, b2, bfin, bsum,
+           sta, a0, a1, afin, stb, b0, b1, bfin,
            in_sem, out_sem, ssem, rsem):
     s = lax.axis_index("seq")
     y = lax.axis_index("head")
@@ -143,6 +149,11 @@
     def along_y(i):
         return {"seq": s, "head": i}
 
+    def chip_at(dx, dz):
+        return {"seq": ((x + dx) % 4 * 4 + (z + dz) % 4) * 2 + c, "head": y}
+
+    others = sorted([(dx, dz) for dx in range(4) for dz in range(4) if dx or dz],
+                    key=lambda place: -sum(min(d, 4 - d) for d in place))
     partner = {"seq": s + 1 - 2 * c, "head": y}
 
     def local(src, dst, sem):
@@ -157,18 +168,17 @@
 
     barrier = pltpu.get_barrier_semaphore()
     peers = [partner, along_y((y + 1) % 4), along_y((y + 3) % 4)]
-    peers += [first((fa + d) % 4) for d in (1, 2, 3)]
-    peers += [second((sa + d) % 4) for d in (1, 2, 3)]
+    peers += [chip_at(*place) for place in others]
     for peer in peers:
         pl.semaphore_signal(barrier, inc=1, device_id=peer, device_id_type=MESH)
 
     copies = Copies(ssem, rsem)
 
     def head(h):
-        return pl.ds(pl.multiple_of(h * HD, 16), HD)
+        return pl.ds(h * HD, HD)
 
     def block(h):
-        return pl.ds(pl.multiple_of(h * HP, HP), HP)
+        return pl.ds(h * HP, HP)
 
     def sum_row(row):
         keep = lax.broadcasted_iota(jnp.int32, (HP - HD, T), 0) == 0
@@ -182,20 +192,20 @@
                 total = value if total is None else total + value
             st[head(h), :] = total
 
-        loop(HEADS, one)
+        each(HEADS, one)
         st[W:SR, :] = jnp.zeros((SR - W, HP), f32)
 
     half = SR // 2
-    piece = half // 4
     mine = pl.multiple_of(c * half, 8)
     other = pl.multiple_of((1 - c) * half, 8)
 
-    def mine_piece(i):
-        return pl.ds(pl.multiple_of(c * half + i * piece, 8), piece)
+    def piece(dx, dz):
+        place = (x + dx) % 4 * 4 + (z + dz) % 4
+        return pl.ds(pl.multiple_of(c * half + place * PR, 8), PR)
 
     class State:
-        def __init__(self, st, r0, r1, r2, fin, total):
-            self.st, self.r0, self.r1, self.r2, self.fin, self.total = st, r0, r1, r2, fin, total
+        def __init__(self, st, r0, r1, fin):
+            self.st, self.r0, self.r1, self.fin = st, r0, r1, fin
 
         def step0(self):
             self.c = copies.start(self.st.at[pl.ds(other, half), :], self.r0, partner)
@@ -204,25 +214,21 @@
             self.c.wait_recv()
             rows = pl.ds(mine, half)
             self.st[rows, :] = self.st[rows, :] + self.r0[...]
-            self.cs = [copies.start(self.st.at[mine_piece((fa + d) % 4), :], self.r1.at[d - 1],
-                                    first((fa + d) % 4)) for d in (1, 2, 3)]
+            self.cs = [copies.start(self.st.at[piece(*place), :], self.r1.at[i], chip_at(*place))
+                       for i, place in enumerate(others)]
 
         def step2(self):
             for copy in self.cs:
                 copy.wait_recv()
-            self.total[...] = (self.st[mine_piece(fa), :] + self.r1[0]) + (self.r1[1] + self.r1[2])
-            self.cs = [copies.start(self.total, self.r2.at[d - 1], second((sa + d) % 4))
-                       for d in (1, 2, 3)]
+            rows = piece(0, 0)
+            total = self.st[rows, :]
+            for i in range(0, NB - 1, 3):
+                total = total + (self.r1[i] + self.r1[i + 1] + self.r1[i + 2])
+            self.fin[rows, :] = total
+            self.cs = [copies.start(self.fin.at[rows, :], self.fin.at[rows, :], chip_at(*place))
+                       for place in others]
 
         def step3(self):
-            for copy in self.cs:
-                copy.wait_recv()
-            rows = mine_piece(fa)
-            self.fin[rows, :] = (self.total[...] + self.r2[0]) + (self.r2[1] + self.r2[2])
-            self.cs = [copies.start(self.fin.at[rows, :], self.fin.at[rows, :], first((fa + d) % 4))
-                       for d in (1, 2, 3)]
-
-        def step4(self):
             for copy in self.cs:
                 copy.wait_recv()
             rows = pl.ds(mine, half)
@@ -243,7 +249,7 @@
     in_o = local(wo_h, wslot.at[1], in_sem.at[5])
     state_part(sta, k, [v])
     pl.semaphore_wait(barrier, len(peers))
-    state = State(sta, a0, a1, a2, afin, asum)
+    state = State(sta, a0, a1, afin)
     state.step0()
 
     in_q.wait()
@@ -275,25 +281,32 @@
         return copies.start(cp.at[place, :], dp.at[place, :], partner)
 
     def flip(src, dst):
-        def columns(start, n):
-            eye = (lax.broadcasted_iota(jnp.int32, (n, n), 0) == lax.broadcasted_iota(jnp.int32, (n, n), 1))
-            dst[pl.ds(start, n), :] = dot_t(
-                eye.astype(f32).astype(bf16), src[:, pl.ds(start, n)]).astype(bf16)
-
-        loop(D // 256, lambda i: columns(pl.multiple_of(i * 256, 256), 256))
-        columns(D // 256 * 256, D % 256)
+        for start in range(0, D, 256):
+            n = min(256, D - start)
+            dst[start:start + n, :] = src[:, start:start + n].T
+
+    def cast_rows(dst, base):
+        def cast(i):
+            r = pl.multiple_of(i * 288, 16)
+            dst[pl.ds(r, 288), T:2 * T] = dp[pl.ds(pl.multiple_of(base + r, 8), 288), :].astype(bf16)
+
+        loop(GR // 288, cast)
 
     send_tok = rows_of(tok, tokt, 0)
-    state.step2()
-
     in_o.wait()
     in_go.wait()
     gm[...] = dot(wslot[1], go[...]).astype(bf16)
-    state.step3()
+    state.step2()
     send_go = rows_of(go, got, GR)
-    state.step4()
     flip(wslot.at[1], wot)
     in_v = local(wv_h, wslot.at[1], in_sem.at[2])
+    send_tok.wait_recv()
+    cast_rows(tokt, 0)
+    state.step3()
+    send_go.wait_recv()
+    cast_rows(got, GR)
+    flip(wslot.at[0], wqn)
+    in_k = local(wk_h, wslot.at[0], in_sem.at[1])
     rhs1[2 * W:GC, :] = jnp.zeros((GC - 2 * W, 2 * T), bf16)
     rhs2[2 * W:GC, :] = jnp.zeros((GC - 2 * W, 2 * T), bf16)
 
@@ -310,15 +323,17 @@
         g = gm[head(h), :].astype(f32)
         grad = -jnp.sum(g * att, axis=0, keepdims=True) * rec
         high, low = parts(g * rec)
-        at = pl.ds(pl.multiple_of(h * HP, HP), HD)
+        at = pl.ds(h * HP, HD)
         ngh[at, :] = high
         ngl[at, :] = low
         high, low = parts(sum_row(grad))
-        at = pl.ds(pl.multiple_of(h * HP + HD, 16), HP - HD)
+        at = pl.ds(h * HP + HD, HP - HD)
         ngh[at, :] = high
         ngl[at, :] = low
 
-    loop(HEADS, attend)
+    each(HEADS, attend)
+    first_half, second_half = pl.ds(0, W), pl.ds(W, W)
+    pair_m = copies.start(send.at[first_half, :], recv.at[first_half, :], partner)
 
     ring_y = {"far": (y + 2) % 4, "right": (y + 1) % 4, "left": (y + 3) % 4, "own": y}
     order = {"far": 0, "right": 1, "left": 2, "own": 3}
@@ -343,80 +358,55 @@
     ring_c.far()
 
     state_part(stb, q, [ngh, ngl])
-    state = State(stb, b0, b1, b2, bfin, bsum)
+    state = State(stb, b0, b1, bfin)
     state.step0()
-    out_chunk("right")
-    ring_c.near_right()
-    out_chunk("left")
-    ring_c.near_left()
-    state.step1()
 
     def query_grad(h):
         high, low = parts(afin[head(h), :])
         ng = ngh[block(h), :]
         value = dot(high, ng) + dot(low, ng) + dot(high, ngl[block(h), :])
         value = jnp.where(q[head(h), :].astype(f32) > 0, value, 0.0).astype(bf16)
-        at = pl.ds(pl.multiple_of(W + h * HD, 16), HD)
+        at = pl.ds(W + h * HD, HD)
         rhs1[at, 0:T] = value
         send[at, :] = value.astype(f32)
 
-    loop(HEADS, query_grad)
-    pair = copies.start(send, recv, partner)
-    state.step2()
-
-    def cast_rows(dst, base):
+    each(HEADS, query_grad)
+    pair_q = copies.start(send.at[second_half, :], recv.at[second_half, :], partner)
+    state.step1()
+
+    def take_pair(dst, base):
         def cast(i):
-            r = pl.multiple_of(i * 288, 16)
-            dst[pl.ds(r, 288), T:2 * T] = dp[pl.ds(pl.multiple_of(base + r, 8), 288), :].astype(bf16)
-
-        loop(GR // 288, cast)
-
-    flip(wslot.at[0], wqn)
-    in_k = local(wk_h, wslot.at[0], in_sem.at[1])
-    send_tok.wait_recv()
-    cast_rows(tokt, 0)
-    send_go.wait_recv()
-    cast_rows(got, GR)
-    state.step3()
-
-    def take_pair(dst):
-        def cast(i):
-            r = pl.ds(pl.multiple_of(i * HD, 16), HD)
+            r = pl.ds(pl.multiple_of(base + i * HD, 16), HD)
             dst[r, T:2 * T] = recv[r, :].astype(bf16)
 
-        loop(2 * W // HD, cast)
-
-    pair.wait_recv()
-    take_pair(rhs1)
-    copies.sent(pair)
+        loop(W // HD, cast)
+
+    pair_m.wait_recv()
+    take_pair(rhs1, 0)
+    pair_q.wait_recv()
+    take_pair(rhs1, W)
 
     ring_f = {"far": (fa + 2) % 4, "right": (fa + 1) % 4, "left": (fa + 3) % 4, "own": fa}
 
-    def tiles_of(which, dst, fn):
+    def chunk_of(which):
+        rows = pl.ds(pl.multiple_of(ring_f[which] * CH, 16), CH)
         base = 0 if which == "own" else order[which] * CH
-
-        def tile(i):
-            rows = pl.ds(pl.multiple_of(ring_f[which] * CH + i * 144, 16), 144)
-            fn(rows, dst, pl.ds(pl.multiple_of(base + i * 144, 16), 144))
-
-        loop(2, tile)
-
-    def first_tile(rows, dst, to):
+        return rows, pl.ds(base, CH)
+
+    def first_pair(which):
+        rows, to = chunk_of(which)
+        dst = own1 if which == "own" else gbuf
         lo, lt = got[rows, :], tokt[rows, :]
         dst[to, 0:512] = dot_t(lo, rhs1[0:512, :])
         shared = rhs1[512:640, :]
-        is_out = lax.broadcasted_iota(jnp.int32, (144, 128), 1) < W - 512
+        is_out = lax.broadcasted_iota(jnp.int32, (CH, 128), 1) < W - 512
         dst[to, 512:640] = jnp.where(is_out, dot_t(lo, shared), dot_t(lt, shared))
         dst[to, 640:GC] = dot_t(lt, rhs1[640:GC, :])
 
-    def second_tile(rows, dst, to):
+    def second_pair(which):
+        rows, to = chunk_of(which)
+        dst = own2 if which == "own" else gbuf
         dst[to, :] = dot_t(tokt[rows, :], rhs2[...])
-
-    def first_pair(which):
-        tiles_of(which, own1 if which == "own" else gbuf, first_tile)
-
-    def second_pair(which):
-        tiles_of(which, own2 if which == "own" else gbuf, second_tile)
 
     def g_slot(which, h):
         return gbuf.at[pl.ds(order[which] * CH + h * 144, 144), :]
@@ -441,16 +431,25 @@
 
     first_pair("far")
     ring_1.far()
-    state.step4()
     first_pair("right")
     ring_1.near_right()
     first_pair("left")
     ring_1.near_left()
-    ring_c.combine()
+    out_chunk("right")
+    ring_c.near_right()
+    out_chunk("left")
+    ring_c.near_left()
+    state.step2()
+    copies.sent(pair_m)
+    copies.sent(pair_q)
+    first_pair("own")
     in_v.wait()
     flip(wslot.at[1], wvn)
+    ring_c.combine()
     in_k.wait()
     flip(wslot.at[0], wkn)
+    state.step3()
+    ring_1.combine()
 
     state.done()
 
@@ -462,11 +461,11 @@
         two = (dot_n(high, kt) + dot_n(low, kt))[0:HD, :].astype(bf16)
         rhs2[head(h), 0:T] = one
         send[head(h), :] = one.astype(f32)
-        at = pl.ds(pl.multiple_of(W + h * HD, 16), HD)
+        at = pl.ds(W + h * HD, HD)
         rhs2[at, 0:T] = two
         send[at, :] = two.astype(f32)
 
-    loop(HEADS, key_value_grad)
+    each(HEADS, key_value_grad)
     pair = copies.start(send, recv, partner)
 
     def in_chunk(which):
@@ -478,18 +477,16 @@
     ring_d = Ring(copies, down, up, y_slot(dp), dbox, W // 2)
     in_chunk("far")
     ring_d.far()
-    ring_1.combine()
     in_chunk("right")
     ring_d.near_right()
-    in_chunk("left")
-    ring_d.near_left()
-
     pair.wait_recv()
-    take_pair(rhs2)
-    first_pair("own")
+    take_pair(rhs2, 0)
+    take_pair(rhs2, W)
     ring_1.sent(("a0", "a1"))
     second_pair("far")
     ring_2.far()
+    in_chunk("left")
+    ring_d.near_left()
     second_pair("own")
     out_chunk("own")
     in_chunk("own")
@@ -526,8 +523,8 @@
     out_c = y_sum(cp, cbox, q, at_o, out_sem.at[0])
 
     ring_2.combine()
+    ring_d.combine()
     ring_p.combine()
-    ring_d.combine()
 
     def final(src, box, out, sem):
         rows = pl.ds(pl.multiple_of(sa * RP, 8), RP)
@@ -553,17 +550,14 @@
         copy.wait()
 
 
-def finish(factor, at, gt, g1, g2, at_o, gt_o, gq_o, gk_o, gv_o, gw_o, sem):
-    copies = [pltpu.make_async_copy(at, at_o, sem.at[0]), pltpu.make_async_copy(gt, gt_o, sem.at[1])]
-    for copy in copies:
-        copy.start()
+def finish(factor, at, gt, g1, g2, at_o, gt_o, gq_o, gk_o, gv_o, gw_o):
+    at_o[...] = at[...]
+    gt_o[...] = gt[...]
     one, two = g1[0:ROWS, :] * factor, g2[0:ROWS, :] * factor
     gw_o[...] = one[:, 0:W]
     gq_o[...] = one[:, W:2 * W]
     gk_o[...] = two[:, 0:W]
     gv_o[...] = two[:, W:2 * W]
-    for copy in copies:
-        copy.wait()
 
 
 def body(tokens, w_query, w_key, w_value, w_out, grad_out):
@@ -579,12 +573,11 @@
         ((2 * GR, T), f32), ((2 * GR, T), f32), ((3, W, T), f32), ((3, W, T), f32),
     ]
     for _ in range(2):
-        shapes += [((SR, HP), f32), ((SR // 2, HP), f32), ((3, RP, HP), f32), ((3, RP, HP), f32),
-                   ((SR, HP), f32), ((RP, HP), f32)]
+        shapes += [((SR, HP), f32), ((SR // 2, HP), f32), ((NB - 1, PR, HP), f32), ((SR, HP), f32)]
     scratch = [pltpu.VMEM(*shape) for shape in shapes]
     scratch += [
         pltpu.SemaphoreType.DMA((6,)), pltpu.SemaphoreType.DMA((4,)),
-        pltpu.SemaphoreType.DMA((64,)), pltpu.SemaphoreType.DMA((64,)),
+        pltpu.SemaphoreType.DMA((112,)), pltpu.SemaphoreType.DMA((112,)),
     ]
     spaces = [pl.BlockSpec(memory_space=pl.ANY)] * 6
     at, gt, g1, g2 = pl.pallas_call(
@@ -610,9 +603,8 @@
             jax.ShapeDtypeStruct((W, T), bf16), jax.ShapeDtypeStruct((W, T), bf16),
             grad, grad, grad, grad,
         ),
-        in_specs=spaces[:2] + [vmem] * 2,
-        out_specs=spaces[:2] + [vmem] * 4,
-        scratch_shapes=[pltpu.SemaphoreType.DMA((2,))],
+        in_specs=[vmem] * 4,
+        out_specs=[vmem] * 6,
         name="final_arrays",
     )(at, gt, g1, g2)
     return (at.T, gt.T, gq, gk, gv, gw.T)

time: 134 us -> 101 us (0.75)
  Pallas kernels: 133 us -> 100 us
    pallas_call x1, Pallas kernels: 29.1 us -> 2.6 us  [body(): pl.pallas_call(functools.partial(finish, factor), out_shape=(jax.ShapeDty...]
    pallas_call x1, Pallas kernels: 103 us -> 97.5 us  [body(): pl.pallas_call(kernel, out_shape=(jax.ShapeDtypeStruct((W, T), bf16), jax...]
where the time goes in v3:
time: 101 us
  Pallas kernels  100 us (99%)
    pallas_call x1, Pallas kernels, body(): pl.pallas_call(kernel, out_shape=(jax.ShapeDtypeStruct((W, T), bf16), jax...  97.5 us
    pallas_call x1, Pallas kernels, body(): pl.pallas_call(functools.partial(finish, factor), out_shape=(jax.ShapeDty...  2.6 us

profile of v3, /device:TPU:0, one launch (start us, length us, event | category | flops | bytes accessed | tf_op | source)
XLA Modules:
  0.0 100.8 jit_solution(16161934081869821948)
XLA Ops:
  0.6 97.5 %fused_attention.1 = (bf16[560,384]{1,0:T(8,128)(2,1)}, bf16[560,384]{1,0:T(8,128)(2,1)}, f32[72,1152]{1,0:T(8,128)}, f32[72,1152]{1,0:T(8,128)}) custom-call(bf16[2240,384]{1,0:T(8,128)(2,1)} %bitcast.11, bf16[560,2240]{1,0:T(8,128)(2,1)} %bitcast.8, bf16[560,2240]{1,0:T(8,128)(2,1)} %bitcast.9, bf16[560,2240]{1,0:T(8,128)(2,1)} %bitcast.10, ...), custom_call_target="tpu_custom_call" | custom-call | flops 16000000000 | bytes 16000000 | tf_op jit(solution)/shard_map/fused_attention/pallas_call | solution.py:583
  98.2 2.6 %final_arrays.1 = (bf16[560,384]{1,0:T(8,128)(2,1)}, bf16[560,384]{1,0:T(8,128)(2,1)}, f32[70,560]{1,0:T(8,128)}, f32[70,560]{1,0:T(8,128)}, f32[70,560]{1,0:T(8,128)}, /*index=5*/f32[70,560]{1,0:T(8,128)}) custom-call(bf16[560,384]{1,0:T(8,128)(2,1)} %get-tuple-element.16.at, bf16[560,384]{1,0:T(8,128)(2,1)} %get-tuple-element.17.gt, ...), custom_call_target="tpu_custom_call" | custom-call | tf_op jit(solution)/shard_map/final_arrays/pallas_call | solution.py:600

commit v4 on v3

--- a/solution.py
+++ b/solution.py
@@ -23,6 +23,7 @@
 NB = 16
 GR = NB * RP
 GC = 1152
+WP = 640
 CH = 4 * RP
 PR = 24
 SR = 2 * NB * PR
@@ -124,10 +125,10 @@
 
 
 def kernel(tok_h, wq_h, wk_h, wv_h, wo_h, go_h,
-           at_o, gt_o, g1_o, g2_o,
+           at_o, gt_o, g1_o, g2_o, g3_o,
            tok, go, wslot, wot, wqn, wkn, wvn, tokt, got,
-           q, k, v, gm, ngh, ngl, rhs1, rhs2, send, recv,
-           gbuf, own1, own2, box1, box2, pbox1, pbox2,
+           q, v, gm, kx, rhs1, rhs2, send, recv,
+           gbuf, tbuf, own1, own2, own3, box1, box2, box3, pbox1, pbox2, pbox3,
            cp, dp, cbox, dbox,
            sta, a0, a1, afin, stb, b0, b1, bfin,
            in_sem, out_sem, ssem, rsem):
@@ -237,25 +238,6 @@
         def done(self):
             self.c.wait_recv()
 
-    in_tok.wait()
-    in_k.wait()
-    k[...] = jnp.maximum(dot(wslot[0], tok[...]), 0.0).astype(bf16)
-    in_q = local(wq_h, wslot.at[0], in_sem.at[4])
-    in_v.wait()
-    value = dot(wslot[1], tok[...]).astype(bf16)
-    for h in range(HEADS):
-        v[HP * h:HP * h + HD, :] = value[HD * h:HD * h + HD, :]
-        v[HP * h + HD:HP * h + HP, :] = sum_row(jnp.ones((1, T), f32)).astype(bf16)
-    in_o = local(wo_h, wslot.at[1], in_sem.at[5])
-    state_part(sta, k, [v])
-    pl.semaphore_wait(barrier, len(peers))
-    state = State(sta, a0, a1, afin)
-    state.step0()
-
-    in_q.wait()
-    q[...] = jnp.maximum(dot(wslot[0], tok[...]), 0.0).astype(bf16)
-    state.step1()
-
     def gather_rows(src, base, which):
         for b in range(NB):
             lo = 2 * ROWS * b
@@ -268,7 +250,7 @@
             cp[pl.ds(pl.multiple_of(base + place * RP, 8), RP), :] = dot(
                 pick.astype(f32).astype(bf16), src[w0:w1, :])
 
-    def rows_of(src, dst, base):
+    def own_rows(src, dst, base):
         gather_rows(src, base, c)
 
         def cast(i):
@@ -276,6 +258,8 @@
             dst[pl.ds(r, 288), 0:T] = cp[pl.ds(pl.multiple_of(base + r, 8), 288), :].astype(bf16)
 
         loop(GR // 288, cast)
+
+    def send_rows(src, base):
         gather_rows(src, base, 1 - c)
         place = pl.ds(base, GR)
         return copies.start(cp.at[place, :], dp.at[place, :], partner)
@@ -292,25 +276,133 @@
 
         loop(GR // 288, cast)
 
-    send_tok = rows_of(tok, tokt, 0)
+    def take_pair(dst, base, source):
+        def cast(i):
+            r = pl.multiple_of(i * HD, 16)
+            dst[pl.ds(base + r, HD), T:2 * T] = recv[pl.ds(source + r, HD), :].astype(bf16)
+
+        loop(W // HD, cast)
+
+    first_half, second_half = pl.ds(0, W), pl.ds(W, W)
+    order = {"far": 0, "right": 1, "left": 2, "own": 3}
+
+    ring_f = {"far": (fa + 2) % 4, "right": (fa + 1) % 4, "left": (fa + 3) % 4, "own": fa}
+    fr, fl = first((fa + 1) % 4), first((fa + 3) % 4)
+    sr, sl = second((sa + 1) % 4), second((sa + 3) % 4)
+
+    def g_slot(buf):
+        def slot(which, h):
+            return buf.at[pl.ds(order[which] * CH + h * 144, 144), :]
+
+        return slot
+
+    def p_slot(buf):
+        far = {"far": (sa + 2) % 4, "right": (sa + 1) % 4, "left": (sa + 3) % 4}
+
+        def slot(which, h):
+            base = far[which] * RP
+            if h == 0:
+                return buf.at[pl.ds(pl.multiple_of(base, 8), 40), :]
+            return buf.at[pl.ds(pl.multiple_of(base + 40, 8), 32), :]
+
+        return slot
+
+    ring_1 = Ring(copies, fl, fr, g_slot(gbuf), box1, 144)
+    ring_2 = Ring(copies, fl, fr, g_slot(tbuf), box2, 144)
+    ring_3 = Ring(copies, fl, fr, g_slot(tbuf), box3, 144)
+    ring_1p = Ring(copies, sl, sr, p_slot(own1), pbox1, 40)
+    ring_2p = Ring(copies, sl, sr, p_slot(own2), pbox2, 40)
+    ring_3p = Ring(copies, sl, sr, p_slot(own3), pbox3, 40)
+
+    def chunk_of(which):
+        rows = pl.ds(pl.multiple_of(ring_f[which] * CH, 16), CH)
+        base = 0 if which == "own" else order[which] * CH
+        return rows, pl.ds(base, CH)
+
+    def first_pair(which):
+        rows, to = chunk_of(which)
+        dst = own1 if which == "own" else gbuf
+        lo, lt = got[rows, :], tokt[rows, :]
+        dst[to, 0:512] = dot_t(lo, rhs1[0:512, :])
+        shared = rhs1[512:640, :]
+        is_out = lax.broadcasted_iota(jnp.int32, (CH, 128), 1) < W - 512
+        dst[to, 512:640] = jnp.where(is_out, dot_t(lo, shared), dot_t(lt, shared))
+        dst[to, 640:GC] = dot_t(lt, rhs1[640:GC, :])
+
+    def key_chunk(which):
+        rows, to = chunk_of(which)
+        dst = own2 if which == "own" else tbuf
+        dst[to, :] = dot_t(tokt[rows, :], rhs2[...])
+
+    def moment_chunk(which):
+        rows, to = chunk_of(which)
+        dst = own3 if which == "own" else tbuf
+        dst[to, :] = dot_t(tokt[rows, :], kx[...])
+
+    def add_up(dst, box, rows, tile):
+        def step(i):
+            r = pl.ds(pl.multiple_of(i * tile, 8), tile)
+            dst[r, :] = dst[r, :] + (box[1, r, :] + box[2, r, :])
+
+        loop(rows // tile, step)
+
+    in_tok.wait()
+    in_k.wait()
+    value = jnp.maximum(dot(wslot[0], tok[...]), 0.0).astype(bf16)
+    k = kx.at[pl.ds(0, W), pl.ds(0, T)]
+    k[...] = value
+    send[first_half, :] = value.astype(f32)
+    in_q = local(wq_h, wslot.at[0], in_sem.at[4])
+    pl.semaphore_wait(barrier, len(peers))
+    pair_k = copies.start(send.at[first_half, :], recv.at[first_half, :], partner)
+    in_v.wait()
+    value = dot(wslot[1], tok[...]).astype(bf16)
+    for h in range(HEADS):
+        v[HP * h:HP * h + HD, :] = value[HD * h:HD * h + HD, :]
+        v[HP * h + HD:HP * h + HP, :] = sum_row(jnp.ones((1, T), f32)).astype(bf16)
+    in_o = local(wo_h, wslot.at[1], in_sem.at[5])
+    state_part(sta, k, [v])
+    state = State(sta, a0, a1, afin)
+    state.step0()
+    send_tok = send_rows(tok, 0)
+
+    in_q.wait()
+    q[...] = jnp.maximum(dot(wslot[0], tok[...]), 0.0).astype(bf16)
+    state.step1()
+    own_rows(tok, tokt, GR)
+    kx[W:WP, :] = jnp.zeros((WP - W, 2 * T), bf16)
+    rhs1[2 * W:GC, :] = jnp.zeros((GC - 2 * W, 2 * T), bf16)
+    rhs2[W:WP, :] = jnp.zeros((WP - W, 2 * T), bf16)
+    pair_k.wait_recv()
+    take_pair(kx, 0, 0)
+    send_tok.wait_recv()
+    cast_rows(tokt, 0)
+    moment_chunk("far")
+    ring_3.far()
+    moment_chunk("right")
+    moment_chunk("left")
     in_o.wait()
     in_go.wait()
     gm[...] = dot(wslot[1], go[...]).astype(bf16)
     state.step2()
-    send_go = rows_of(go, got, GR)
+    ring_3.near_right()
+    ring_3.near_left()
+    ring_3.combine()
+    send_go = send_rows(go, GR)
     flip(wslot.at[1], wot)
     in_v = local(wv_h, wslot.at[1], in_sem.at[2])
-    send_tok.wait_recv()
-    cast_rows(tokt, 0)
+    copies.sent(send_tok)
+    own_rows(go, got, 0)
+    moment_chunk("own")
     state.step3()
     send_go.wait_recv()
     cast_rows(got, GR)
     flip(wslot.at[0], wqn)
     in_k = local(wk_h, wslot.at[0], in_sem.at[1])
-    rhs1[2 * W:GC, :] = jnp.zeros((GC - 2 * W, 2 * T), bf16)
-    rhs2[2 * W:GC, :] = jnp.zeros((GC - 2 * W, 2 * T), bf16)
-
+    copies.sent(pair_k)
     state.done()
+
+    dv, ngh, ngl = (tok.at[pl.ds(WP * i, WP), :] for i in range(3))
 
     def attend(h):
         high, low = parts(afin[head(h), :])
@@ -332,12 +424,9 @@
         ngl[at, :] = low
 
     each(HEADS, attend)
-    first_half, second_half = pl.ds(0, W), pl.ds(W, W)
     pair_m = copies.start(send.at[first_half, :], recv.at[first_half, :], partner)
 
     ring_y = {"far": (y + 2) % 4, "right": (y + 1) % 4, "left": (y + 3) % 4, "own": y}
-    order = {"far": 0, "right": 1, "left": 2, "own": 3}
-    copies.sent(send_tok)
     copies.sent(send_go)
 
     def y_rows(which):
@@ -373,81 +462,35 @@
     each(HEADS, query_grad)
     pair_q = copies.start(send.at[second_half, :], recv.at[second_half, :], partner)
     state.step1()
-
-    def take_pair(dst, base):
-        def cast(i):
-            r = pl.ds(pl.multiple_of(base + i * HD, 16), HD)
-            dst[r, T:2 * T] = recv[r, :].astype(bf16)
-
-        loop(W // HD, cast)
-
+    ring_3.arrived()
+    add_up(own3, box3, CH, 96)
+    ring_3p.far()
+    ring_3p.near_right()
+    ring_3p.near_left()
     pair_m.wait_recv()
-    take_pair(rhs1, 0)
+    take_pair(rhs1, 0, 0)
     pair_q.wait_recv()
-    take_pair(rhs1, W)
-
-    ring_f = {"far": (fa + 2) % 4, "right": (fa + 1) % 4, "left": (fa + 3) % 4, "own": fa}
-
-    def chunk_of(which):
-        rows = pl.ds(pl.multiple_of(ring_f[which] * CH, 16), CH)
-        base = 0 if which == "own" else order[which] * CH
-        return rows, pl.ds(base, CH)
-
-    def first_pair(which):
-        rows, to = chunk_of(which)
-        dst = own1 if which == "own" else gbuf
-        lo, lt = got[rows, :], tokt[rows, :]
-        dst[to, 0:512] = dot_t(lo, rhs1[0:512, :])
-        shared = rhs1[512:640, :]
-        is_out = lax.broadcasted_iota(jnp.int32, (CH, 128), 1) < W - 512
-        dst[to, 512:640] = jnp.where(is_out, dot_t(lo, shared), dot_t(lt, shared))
-        dst[to, 640:GC] = dot_t(lt, rhs1[640:GC, :])
-
-    def second_pair(which):
-        rows, to = chunk_of(which)
-        dst = own2 if which == "own" else gbuf
-        dst[to, :] = dot_t(tokt[rows, :], rhs2[...])
-
-    def g_slot(which, h):
-        return gbuf.at[pl.ds(order[which] * CH + h * 144, 144), :]
-
-    def p_slot(buf):
-        far = {"far": (sa + 2) % 4, "right": (sa + 1) % 4, "left": (sa + 3) % 4}
-
-        def slot(which, h):
-            base = far[which] * RP
-            if h == 0:
-                return buf.at[pl.ds(pl.multiple_of(base, 8), 40), :]
-            return buf.at[pl.ds(pl.multiple_of(base + 40, 8), 32), :]
-
-        return slot
-
-    fr, fl = first((fa + 1) % 4), first((fa + 3) % 4)
-    sr, sl = second((sa + 1) % 4), second((sa + 3) % 4)
-    ring_1 = Ring(copies, fl, fr, g_slot, box1, 144)
-    ring_2 = Ring(copies, fl, fr, g_slot, box2, 144)
-    ring_p = Ring(copies, sl, sr, p_slot(own1), pbox1, 40)
-    ring_r = Ring(copies, sl, sr, p_slot(own2), pbox2, 40)
-
+    take_pair(rhs1, W, W)
     first_pair("far")
     ring_1.far()
-    first_pair("right")
-    ring_1.near_right()
-    first_pair("left")
-    ring_1.near_left()
     out_chunk("right")
     ring_c.near_right()
     out_chunk("left")
     ring_c.near_left()
+    first_pair("right")
+    first_pair("left")
     state.step2()
+    ring_1.near_right()
+    ring_1.near_left()
     copies.sent(pair_m)
     copies.sent(pair_q)
-    first_pair("own")
+    ring_3p.combine()
     in_v.wait()
     flip(wslot.at[1], wvn)
-    ring_c.combine()
     in_k.wait()
     flip(wslot.at[0], wkn)
+    ring_c.combine()
+    first_pair("own")
     state.step3()
     ring_1.combine()
 
@@ -458,57 +501,59 @@
         kt, vt = k[head(h), :], v[block(h), :]
         one = dot(high, vt) + dot(low, vt)
         one = jnp.where(kt.astype(f32) > 0, one, 0.0).astype(bf16)
-        two = (dot_n(high, kt) + dot_n(low, kt))[0:HD, :].astype(bf16)
         rhs2[head(h), 0:T] = one
         send[head(h), :] = one.astype(f32)
-        at = pl.ds(W + h * HD, HD)
-        rhs2[at, 0:T] = two
-        send[at, :] = two.astype(f32)
+        dv[head(h), :] = (dot_n(high, kt) + dot_n(low, kt))[0:HD, :].astype(bf16)
 
     each(HEADS, key_value_grad)
-    pair = copies.start(send, recv, partner)
+    pair = copies.start(send.at[first_half, :], recv.at[first_half, :], partner)
 
     def in_chunk(which):
         rows = y_rows(which)
         dp[pl.ds(order[which] * W, W), :] = (
             dot(wqn[rows, :], rhs1[W:2 * W, 0:T]) + dot(wkn[rows, :], rhs2[0:W, 0:T])
-            + dot(wvn[rows, :], rhs2[W:2 * W, 0:T]))
+            + dot(wvn[rows, :], dv[0:W, :]))
 
     ring_d = Ring(copies, down, up, y_slot(dp), dbox, W // 2)
     in_chunk("far")
     ring_d.far()
+    pair.wait_recv()
+    take_pair(rhs2, 0, 0)
+    ring_3.sent(("a0", "a1", "d0", "d1", "c0", "c1"))
+    key_chunk("far")
+    ring_2.far()
     in_chunk("right")
     ring_d.near_right()
-    pair.wait_recv()
-    take_pair(rhs2, 0)
-    take_pair(rhs2, W)
-    ring_1.sent(("a0", "a1"))
-    second_pair("far")
-    ring_2.far()
     in_chunk("left")
     ring_d.near_left()
-    second_pair("own")
+    key_chunk("right")
+    ring_2.near_right()
+    key_chunk("left")
+    ring_2.near_left()
+    key_chunk("own")
     out_chunk("own")
     in_chunk("own")
 
-    ring_1.sent(("d0", "d1", "c0", "c1"))
-    second_pair("right")
-    ring_2.near_right()
-    second_pair("left")
-    ring_2.near_left()
-
-    def add_up(dst, box, rows, tile):
-        def step(i):
-            r = pl.ds(pl.multiple_of(i * tile, 8), tile)
-            dst[r, :] = dst[r, :] + (box[1, r, :] + box[2, r, :])
-
-        loop(rows // tile, step)
+    def final(src, box, out, sem):
+        rows = pl.ds(pl.multiple_of(sa * RP, 8), RP)
+        src[rows, :] = src[rows, :] + (box[1] + box[2])
+        return local(src.at[rows, :], out, sem)
+
+    ring_3p.arrived()
+    rows = pl.ds(pl.multiple_of(sa * RP, 8), RP)
+    moment = own3[rows, :] + (pbox3[1] + pbox3[2])
+    for h in range(HEADS):
+        high, low = parts(moment[:, HD * h:HD * h + HD])
+        state_high, state_low = parts(bfin[head(h), 0:HD])
+        pbox3[0, :, HD * h:HD * h + HD] = (
+            dot(high, state_high) + dot(high, state_low) + dot(low, state_high))
+    out_3 = local(pbox3.at[0], g3_o, out_sem.at[4])
 
     ring_1.arrived()
     add_up(own1, box1, CH, 96)
-    ring_p.far()
-    ring_p.near_right()
-    ring_p.near_left()
+    ring_1p.far()
+    ring_1p.near_right()
+    ring_1p.near_left()
 
     def y_sum(buf, box, dst, out, sem):
         def step(i):
@@ -524,40 +569,33 @@
 
     ring_2.combine()
     ring_d.combine()
-    ring_p.combine()
-
-    def final(src, box, out, sem):
-        rows = pl.ds(pl.multiple_of(sa * RP, 8), RP)
-        src[rows, :] = src[rows, :] + (box[1] + box[2])
-        return local(src.at[rows, :], out, sem)
-
-    ring_p.arrived()
-    out_1 = final(own1, pbox1, g1_o, out_sem.at[1])
-
+    ring_1p.combine()
     ring_2.arrived()
     add_up(own2, box2, CH, 96)
-    ring_r.far()
-    ring_r.near_right()
-    ring_r.near_left()
-    ring_r.combine()
-    ring_r.arrived()
+    ring_2p.far()
+    ring_2p.near_right()
+    ring_2p.near_left()
+    ring_1p.arrived()
+    out_1 = final(own1, pbox1, g1_o, out_sem.at[1])
+    ring_2p.combine()
+    ring_2p.arrived()
     out_2 = final(own2, pbox2, g2_o, out_sem.at[2])
 
     ring_d.arrived()
     out_d = y_sum(dp, dbox, gm, gt_o, out_sem.at[3])
     copies.finish()
-    for copy in (out_c, out_1, out_2, out_d):
+    for copy in (out_c, out_1, out_2, out_3, out_d):
         copy.wait()
 
 
-def finish(factor, at, gt, g1, g2, at_o, gt_o, gq_o, gk_o, gv_o, gw_o):
+def finish(factor, at, gt, g1, g2, g3, at_o, gt_o, gq_o, gk_o, gv_o, gw_o):
     at_o[...] = at[...]
     gt_o[...] = gt[...]
-    one, two = g1[0:ROWS, :] * factor, g2[0:ROWS, :] * factor
+    one = g1[0:ROWS, :] * factor
     gw_o[...] = one[:, 0:W]
     gq_o[...] = one[:, W:2 * W]
-    gk_o[...] = two[:, 0:W]
-    gv_o[...] = two[:, W:2 * W]
+    gk_o[...] = g2[0:ROWS, 0:W] * factor
+    gv_o[...] = g3[0:ROWS, 0:W] * factor
 
 
 def body(tokens, w_query, w_key, w_value, w_out, grad_out):
@@ -565,29 +603,30 @@
         ((D, T), bf16), ((D, T), bf16), ((2, W, D), bf16),
         ((D, W), bf16), ((D, W), bf16), ((D, W), bf16), ((D, W), bf16),
         ((GR, 2 * T), bf16), ((GR, 2 * T), bf16),
-        ((W, T), bf16), ((W, T), bf16), ((HEADS * HP, T), bf16), ((W, T), bf16),
-        ((HEADS * HP, T), bf16), ((HEADS * HP, T), bf16),
-        ((GC, 2 * T), bf16), ((GC, 2 * T), bf16), ((2 * W, T), f32), ((2 * W, T), f32),
-        ((3 * CH, GC), f32), ((CH, GC), f32), ((CH, GC), f32),
-        ((3, CH, GC), f32), ((3, CH, GC), f32), ((3, RP, GC), f32), ((3, RP, GC), f32),
+        ((W, T), bf16), ((HEADS * HP, T), bf16), ((W, T), bf16), ((WP, 2 * T), bf16),
+        ((GC, 2 * T), bf16), ((WP, 2 * T), bf16), ((2 * W, T), f32), ((2 * W, T), f32),
+        ((3 * CH, GC), f32), ((3 * CH, WP), f32), ((CH, GC), f32), ((CH, WP), f32), ((CH, WP), f32),
+        ((3, CH, GC), f32), ((3, CH, WP), f32), ((3, CH, WP), f32),
+        ((3, RP, GC), f32), ((3, RP, WP), f32), ((3, RP, WP), f32),
         ((2 * GR, T), f32), ((2 * GR, T), f32), ((3, W, T), f32), ((3, W, T), f32),
     ]
     for _ in range(2):
         shapes += [((SR, HP), f32), ((SR // 2, HP), f32), ((NB - 1, PR, HP), f32), ((SR, HP), f32)]
     scratch = [pltpu.VMEM(*shape) for shape in shapes]
     scratch += [
-        pltpu.SemaphoreType.DMA((6,)), pltpu.SemaphoreType.DMA((4,)),
-        pltpu.SemaphoreType.DMA((112,)), pltpu.SemaphoreType.DMA((112,)),
+        pltpu.SemaphoreType.DMA((6,)), pltpu.SemaphoreType.DMA((5,)),
+        pltpu.SemaphoreType.DMA((120,)), pltpu.SemaphoreType.DMA((120,)),
     ]
     spaces = [pl.BlockSpec(memory_space=pl.ANY)] * 6
-    at, gt, g1, g2 = pl.pallas_call(
+    at, gt, g1, g2, g3 = pl.pallas_call(
         kernel,
         out_shape=(
             jax.ShapeDtypeStruct((W, T), bf16), jax.ShapeDtypeStruct((W, T), bf16),
-            jax.ShapeDtypeStruct((RP, GC), f32), jax.ShapeDtypeStruct((RP, GC), f32),
+            jax.ShapeDtypeStruct((RP, GC), f32), jax.ShapeDtypeStruct((RP, WP), f32),
+            jax.ShapeDtypeStruct((RP, WP), f32),
         ),
         in_specs=spaces,
-        out_specs=spaces[:4],
+        out_specs=spaces[:5],
         scratch_shapes=scratch,
         compiler_params=pltpu.CompilerParams(
             collective_id=0, has_side_effects=True, vmem_limit_bytes=64 * 1024 * 1024 - 65536),
@@ -603,10 +642,10 @@
             jax.ShapeDtypeStruct((W, T), bf16), jax.ShapeDtypeStruct((W, T), bf16),
             grad, grad, grad, grad,
         ),
-        in_specs=[vmem] * 4,
+        in_specs=[vmem] * 5,
         out_specs=[vmem] * 6,
         name="final_arrays",
-    )(at, gt, g1, g2)
+    )(at, gt, g1, g2, g3)
     return (at.T, gt.T, gq, gk, gv, gw.T)
 
 

time: 101 us -> 92.7 us (0.918)
  Pallas kernels: 100 us -> 91.8 us
    pallas_call x1, Pallas kernels: 97.5 us -> 89.2 us  [body(): pl.pallas_call(kernel, out_shape=(jax.ShapeDtypeStruct((W, T), bf16), jax...]
where the time goes in v4:
time: 92.7 us; the launch traced here: 92.4 us
  Pallas kernels  91.8 us (99%)
    pallas_call x1, Pallas kernels, body(): pl.pallas_call(kernel, out_shape=(jax.ShapeDtypeStruct((W, T), bf16), jax...  89.2 us
    pallas_call x1, Pallas kernels, body(): pl.pallas_call(functools.partial(finish, factor), out_shape=(jax.ShapeDty...  2.57 us

profile of v4, /device:TPU:0, one launch (start us, length us, event | category | flops | bytes accessed | tf_op | source)
XLA Modules:
  0.0 92.4 jit_solution(4550824303911877444)
XLA Ops:
  0.6 89.2 %fused_attention.1 = (bf16[560,384]{1,0:T(8,128)(2,1)}, bf16[560,384]{1,0:T(8,128)(2,1)}, f32[72,1152]{1,0:T(8,128)}, f32[72,640]{1,0:T(8,128)}, f32[72,640]{1,0:T(8,128)}) custom-call(bf16[2240,384]{1,0:T(8,128)(2,1)} %bitcast.11, bf16[560,2240]{1,0:T(8,128)(2,1)} %bitcast.8, bf16[560,2240]{1,0:T(8,128)(2,1)} %bitcast.9, bf16[560,2240]{1,0:T(8,128)(2,1)} %bitcast.10, ...), custom_call_target="tpu_custom_call" | custom-call | flops 16000000000 | bytes 16000000 | tf_op jit(solution)/shard_map/fused_attention/pallas_call | solution.py:621
  89.9 2.6 %final_arrays.1 = (bf16[560,384]{1,0:T(8,128)(2,1)}, bf16[560,384]{1,0:T(8,128)(2,1)}, f32[70,560]{1,0:T(8,128)}, f32[70,560]{1,0:T(8,128)}, f32[70,560]{1,0:T(8,128)}, /*index=5*/f32[70,560]{1,0:T(8,128)}) custom-call(bf16[560,384]{1,0:T(8,128)(2,1)} %get-tuple-element.17.at, bf16[560,384]{1,0:T(8,128)(2,1)} %get-tuple-element.18.gt, ...), custom_call_target="tpu_custom_call" | custom-call | tf_op jit(solution)/shard_map/final_arrays/pallas_call | solution.py:639

commit v5 on v4

--- a/solution.py
+++ b/solution.py
@@ -379,13 +379,13 @@
     cast_rows(tokt, 0)
     moment_chunk("far")
     ring_3.far()
-    moment_chunk("right")
-    moment_chunk("left")
     in_o.wait()
     in_go.wait()
     gm[...] = dot(wslot[1], go[...]).astype(bf16)
     state.step2()
+    moment_chunk("right")
     ring_3.near_right()
+    moment_chunk("left")
     ring_3.near_left()
     ring_3.combine()
     send_go = send_rows(go, GR)
@@ -490,9 +490,9 @@
     in_k.wait()
     flip(wslot.at[0], wkn)
     ring_c.combine()
+    ring_1.combine()
     first_pair("own")
     state.step3()
-    ring_1.combine()
 
     state.done()
 

time: 92.7 us -> 92.6 us (level)
  no operation moved by 1% of the time
where the time goes in v5:
time: 92.6 us; the launch traced here: 92.4 us
  Pallas kernels  91.8 us (99%)
    pallas_call x1, Pallas kernels, body(): pl.pallas_call(kernel, out_shape=(jax.ShapeDtypeStruct((W, T), bf16), jax...  89.2 us
    pallas_call x1, Pallas kernels, body(): pl.pallas_call(functools.partial(finish, factor), out_shape=(jax.ShapeDty...  2.57 us

profile of v5, /device:TPU:0, one launch (start us, length us, event | category | flops | bytes accessed | tf_op | source)
XLA Modules:
  0.0 92.4 jit_solution(17745034094796978153)
XLA Ops:
  0.6 89.2 %fused_attention.1 = (bf16[560,384]{1,0:T(8,128)(2,1)}, bf16[560,384]{1,0:T(8,128)(2,1)}, f32[72,1152]{1,0:T(8,128)}, f32[72,640]{1,0:T(8,128)}, f32[72,640]{1,0:T(8,128)}) custom-call(bf16[2240,384]{1,0:T(8,128)(2,1)} %bitcast.11, bf16[560,2240]{1,0:T(8,128)(2,1)} %bitcast.8, bf16[560,2240]{1,0:T(8,128)(2,1)} %bitcast.9, bf16[560,2240]{1,0:T(8,128)(2,1)} %bitcast.10, ...), custom_call_target="tpu_custom_call" | custom-call | flops 16000000000 | bytes 16000000 | tf_op jit(solution)/shard_map/fused_attention/pallas_call | solution.py:621
  89.9 2.6 %final_arrays.1 = (bf16[560,384]{1,0:T(8,128)(2,1)}, bf16[560,384]{1,0:T(8,128)(2,1)}, f32[70,560]{1,0:T(8,128)}, f32[70,560]{1,0:T(8,128)}, f32[70,560]{1,0:T(8,128)}, /*index=5*/f32[70,560]{1,0:T(8,128)}) custom-call(bf16[560,384]{1,0:T(8,128)(2,1)} %get-tuple-element.17.at, bf16[560,384]{1,0:T(8,128)(2,1)} %get-tuple-element.18.gt, ...), custom_call_target="tpu_custom_call" | custom-call | tf_op jit(solution)/shard_map/final_arrays/pallas_call | solution.py:639
